TPU v7x, 32 devices: a whole 2x2x4 slice. The times are simulated.
32 devices in a mesh: rep: 4 (over z), exp: 8 (over y, x, core).
Axes of the slice: x: 2, y: 2, z: 4, core: 2. Of those that a mesh axis runs over, the one named last changes fastest.
Arguments:
- inputs: bfloat16 [32, 1024, 1024], P(('rep', 'exp')), may hold values from -6 to 6
- cotangent: bfloat16 [32, 1024, 1024], P(('rep', 'exp')), may hold values from -6 to 6
- token_ids: int32 [32, 1024], P(('rep', 'exp')), may hold values from 0 to 8007
- lengths: int32 [32], P(('rep', 'exp')), may hold values from 1 to 1024, 20480 in all
- hash_table: int32 [8008], replicated, may hold values from 0 to 7
- first_gain: float32 [1024], replicated, may hold values from 0.1 to 1.9
- first_shift: float32 [1024], replicated, may hold values from -3 to 3
- w_query: bfloat16 [1024, 1024], replicated, may hold values from -0.1875 to 0.1875
- w_key: bfloat16 [1024, 1024], replicated, may hold values from -0.1875 to 0.1875
- w_value: bfloat16 [1024, 1024], replicated, may hold values from -0.1875 to 0.1875
- w_output: bfloat16 [1024, 1024], replicated, may hold values from -0.75 to 0.75
- second_gain: float32 [1024], replicated, may hold values from 0.1 to 1.9
- second_shift: float32 [1024], replicated, may hold values from -3 to 3
- expert_in: bfloat16 [8, 4096, 1024], P('exp'), may hold values from -0.1875 to 0.1875
- expert_out: bfloat16 [8, 4096, 1024], P('exp'), may hold values from -0.09375 to 0.09375
Outputs:
- outputs: bfloat16 [32, 1024, 1024], P(('rep', 'exp'))
- grad_inputs: float32 [32, 1024, 1024], P(('rep', 'exp'))
- grad_first_gain: float32 [1024], P(('rep', 'exp'))
- grad_first_shift: float32 [1024], P(('rep', 'exp'))
- grad_query: float32 [1024, 1024], P(('rep', 'exp'))
- grad_key: float32 [1024, 1024], P(('rep', 'exp'))
- grad_value: float32 [1024, 1024], P(('rep', 'exp'))
- grad_output: float32 [1024, 1024], P(('rep', 'exp'))
- grad_second_gain: float32 [1024], P(('rep', 'exp'))
- grad_second_shift: float32 [1024], P(('rep', 'exp'))
- grad_expert_in: float32 [8, 4096, 1024], P('exp', 'rep')
- grad_expert_out: float32 [8, 4096, 1024], P('exp', 'rep')
All inputs are finite; a program needn't handle non-finite values. No bound on the sum of `lengths` on one device may be relied on, other than what follows from the above.
Results may differ from a plain program's by a relative error of at most 0.012.
Values may be sent and summed in bfloat16 or wider, within the bound.
A program may use at most 448 MiB of HBM per device.

v0:
```python
import math

import jax
import jax.numpy as jnp
from jax import lax
from jax.sharding import PartitionSpec as P

HEADS = 16
HEAD_DIM = 64


epsilon = 1e-05


def dot_float(left, right):
    return jnp.dot(left, right, preferred_element_type=jnp.float32)


def gelu_slope(hidden):
    return 0.5 * (1.0 + lax.erf(hidden * (1.0 / math.sqrt(2.0)))) + hidden * jnp.exp(
        -0.5 * hidden * hidden
    ) * (1.0 / math.sqrt(2.0 * math.pi))


def norm_forward(values_in, gain_vec, shift_vec):
    average = jnp.mean(values_in, axis=1, keepdims=True)
    centered = values_in - average
    spread = jnp.mean(centered * centered, axis=1, keepdims=True)
    inverse = lax.rsqrt(spread + epsilon)
    normal = centered * inverse
    return (normal * gain_vec + shift_vec, normal, inverse)


def norm_backward(grad_out, normal, inverse, gain_vec):
    grad_normal = grad_out * gain_vec
    inner = (
        grad_normal
        - jnp.mean(grad_normal, axis=1, keepdims=True)
        - normal * jnp.mean(grad_normal * normal, axis=1, keepdims=True)
    )
    return (inner * inverse, jnp.sum(grad_out * normal, axis=0), jnp.sum(grad_out, axis=0))


def score_block(query_blk, key_rows, allowed):
    scale_factor = query_blk.shape[2] ** (-0.5)
    scores = (
        jnp.einsum("qhd,khd->hqk", query_blk, key_rows, preferred_element_type=jnp.float32)
        * scale_factor
    )
    return jnp.where(allowed[None], scores, -1e30)


def attend_forward(packed):
    query_rows, key_rows, value_rows, length = packed
    seq_len = query_rows.shape[0]
    block_rows = min(512, seq_len)
    places = jnp.arange(seq_len, dtype=jnp.int32)
    outputs = []
    log_parts = []
    for offset in range(0, seq_len, block_rows):
        query_blk = query_rows[offset : offset + block_rows]
        allowed = (places[None, :] <= places[offset : offset + block_rows, None]) & (
            places[None, :] < length
        )
        scores = score_block(query_blk, key_rows, allowed)
        highest = jnp.max(scores, axis=2, keepdims=True)
        powers = jnp.exp(scores - highest)
        summed = jnp.sum(powers, axis=2, keepdims=True)
        shares = (powers / summed).astype(jnp.bfloat16)
        outputs.append(
            jnp.einsum("hqk,khd->qhd", shares, value_rows, preferred_element_type=jnp.float32)
        )
        log_parts.append(highest[:, :, 0] + jnp.log(summed[:, :, 0]))
    return (
        jnp.concatenate(outputs, axis=0).astype(jnp.bfloat16),
        jnp.concatenate(log_parts, axis=1),
    )


def attend_backward(packed):
    query_rows, key_rows, value_rows, length, log_total, grad_mixed = packed
    seq_len = query_rows.shape[0]
    block_rows = min(512, seq_len)
    scale_factor = query_rows.shape[2] ** (-0.5)
    places = jnp.arange(seq_len, dtype=jnp.int32)
    grad_keys = jnp.zeros(key_rows.shape, jnp.float32)
    grad_values = jnp.zeros(value_rows.shape, jnp.float32)
    grad_queries = []
    for offset in range(0, seq_len, block_rows):
        query_blk = query_rows[offset : offset + block_rows]
        grad_blk = grad_mixed[offset : offset + block_rows]
        allowed = (places[None, :] <= places[offset : offset + block_rows, None]) & (
            places[None, :] < length
        )
        scores = score_block(query_blk, key_rows, allowed)
        shares = jnp.where(
            allowed[None], jnp.exp(scores - log_total[:, offset : offset + block_rows, None]), 0.0
        )
        grad_shares = jnp.einsum(
            "qhd,khd->hqk", grad_blk, value_rows, preferred_element_type=jnp.float32
        )
        row_delta = jnp.sum(shares * grad_shares, axis=2, keepdims=True)
        grad_scores = (shares * (grad_shares - row_delta)).astype(jnp.bfloat16)
        grad_queries.append(
            jnp.einsum("hqk,khd->qhd", grad_scores, key_rows, preferred_element_type=jnp.float32)
            * scale_factor
        )
        grad_keys = (
            grad_keys
            + jnp.einsum("hqk,qhd->khd", grad_scores, query_blk, preferred_element_type=jnp.float32)
            * scale_factor
        )
        grad_values = grad_values + jnp.einsum(
            "hqk,qhd->khd",
            shares.astype(jnp.bfloat16),
            grad_blk,
            preferred_element_type=jnp.float32,
        )
    grad_query_rows = jnp.concatenate(grad_queries, axis=0).astype(jnp.bfloat16)
    return (grad_query_rows, grad_keys.astype(jnp.bfloat16), grad_values.astype(jnp.bfloat16))


def body(
    inputs,
    cotangent,
    token_ids,
    lengths,
    hash_table,
    first_gain,
    first_shift,
    w_query,
    w_key,
    w_value,
    w_output,
    second_gain,
    second_shift,
    expert_in,
    expert_out,
):
    seq_count, seq_len, width = inputs.shape
    row_count = seq_count * seq_len
    groups = lax.axis_size("exp")
    capacity = row_count // groups
    slot_total = groups * capacity
    places = jnp.arange(seq_len, dtype=jnp.int32)
    valid = (places[None, :] < lengths[:, None]).reshape(row_count)
    residual = inputs.reshape(row_count, width).astype(jnp.float32)
    grad_final = cotangent.reshape(row_count, width).astype(jnp.float32) * valid[:, None].astype(
        jnp.float32
    )
    expert_of = hash_table[token_ids.reshape(row_count)]
    chosen = (
        (expert_of[:, None] == jnp.arange(groups, dtype=jnp.int32)[None, :]) & valid[:, None]
    ).astype(jnp.int32)
    before = jnp.cumsum(chosen, axis=0) - chosen
    slot_of = jnp.sum(before * chosen, axis=1)
    kept = valid & (slot_of < capacity)
    place = jnp.where(kept, expert_of * capacity + slot_of, slot_total)
    normed_first, normal_first, inverse_first = norm_forward(residual, first_gain, first_shift)
    normed_low = normed_first.astype(jnp.bfloat16)
    shaped = (seq_count, seq_len, HEADS, HEAD_DIM)
    query_rows = dot_float(normed_low, w_query).astype(jnp.bfloat16).reshape(shaped)
    key_rows = dot_float(normed_low, w_key).astype(jnp.bfloat16).reshape(shaped)
    value_rows = dot_float(normed_low, w_value).astype(jnp.bfloat16).reshape(shaped)
    mixed, log_total = lax.map(attend_forward, (query_rows, key_rows, value_rows, lengths))
    mixed_rows = mixed.reshape(row_count, width)
    middle = residual + dot_float(mixed_rows, w_output)
    normed_second, normal_second, inverse_second = norm_forward(middle, second_gain, second_shift)
    send_rows = (
        jnp.zeros((slot_total, width), jnp.bfloat16)
        .at[place]
        .set(normed_second.astype(jnp.bfloat16), mode="drop")
    )
    arrived = lax.all_to_all(
        send_rows.reshape(groups, capacity, width), "exp", split_axis=0, concat_axis=0, tiled=True
    ).reshape(slot_total, width)
    weight_in = expert_in[0]
    weight_out = expert_out[0]
    hidden = jnp.einsum("rd,fd->rf", arrived, weight_in, preferred_element_type=jnp.float32)
    activated = jax.nn.gelu(hidden, approximate=False).astype(jnp.bfloat16)
    expert_result = dot_float(activated, weight_out).astype(jnp.bfloat16)
    returned = lax.all_to_all(
        expert_result.reshape(groups, capacity, width),
        "exp",
        split_axis=0,
        concat_axis=0,
        tiled=True,
    ).reshape(slot_total, width)
    combined = returned.at[place].get(mode="fill", fill_value=0).astype(jnp.float32)
    outputs = (middle + combined).astype(jnp.bfloat16)
    grad_send = (
        jnp.zeros((slot_total, width), jnp.bfloat16)
        .at[place]
        .set(grad_final.astype(jnp.bfloat16), mode="drop")
    )
    grad_arrived = lax.all_to_all(
        grad_send.reshape(groups, capacity, width), "exp", split_axis=0, concat_axis=0, tiled=True
    ).reshape(slot_total, width)
    grad_activated = jnp.einsum(
        "re,fe->rf", grad_arrived, weight_out, preferred_element_type=jnp.float32
    )
    grad_hidden = (grad_activated * gelu_slope(hidden)).astype(jnp.bfloat16)
    grad_in_full = jnp.einsum("rf,rd->fd", grad_hidden, arrived, preferred_element_type=jnp.float32)
    grad_out_full = jnp.einsum(
        "rf,re->fe", activated, grad_arrived, preferred_element_type=jnp.float32
    )
    grad_slots = dot_float(grad_hidden, weight_in)
    grad_expert_in, grad_expert_out = (
        lax.psum_scatter(
            grad_in_full[None].astype(jnp.bfloat16), "rep", scatter_dimension=1, tiled=True
        ).astype(jnp.float32),
        lax.psum_scatter(
            grad_out_full[None].astype(jnp.bfloat16), "rep", scatter_dimension=1, tiled=True
        ).astype(jnp.float32),
    )
    grad_back = lax.all_to_all(
        grad_slots.astype(jnp.bfloat16).reshape(groups, capacity, width),
        "exp",
        split_axis=0,
        concat_axis=0,
        tiled=True,
    ).reshape(slot_total, width)
    grad_sent = grad_back.at[place].get(mode="fill", fill_value=0).astype(jnp.float32)
    grad_norm_mid, grad_second_gain, grad_second_shift = norm_backward(
        grad_sent, normal_second, inverse_second, second_gain
    )
    grad_middle = grad_final + grad_norm_mid
    grad_branch = grad_middle.astype(jnp.bfloat16)
    grad_w_output = jnp.einsum(
        "rd,re->de", mixed_rows, grad_branch, preferred_element_type=jnp.float32
    )
    grad_mixed = jnp.einsum(
        "re,de->rd", grad_branch, w_output, preferred_element_type=jnp.float32
    ).astype(jnp.bfloat16)
    grad_q, grad_k, grad_v = lax.map(
        attend_backward,
        (query_rows, key_rows, value_rows, lengths, log_total, grad_mixed.reshape(shaped)),
    )
    grad_q = grad_q.reshape(row_count, width)
    grad_k = grad_k.reshape(row_count, width)
    grad_v = grad_v.reshape(row_count, width)
    grad_w_query = jnp.einsum("rd,re->de", normed_low, grad_q, preferred_element_type=jnp.float32)
    grad_w_key = jnp.einsum("rd,re->de", normed_low, grad_k, preferred_element_type=jnp.float32)
    grad_w_value = jnp.einsum("rd,re->de", normed_low, grad_v, preferred_element_type=jnp.float32)
    grad_normed = (
        jnp.einsum("re,de->rd", grad_q, w_query, preferred_element_type=jnp.float32)
        + jnp.einsum("re,de->rd", grad_k, w_key, preferred_element_type=jnp.float32)
        + jnp.einsum("re,de->rd", grad_v, w_value, preferred_element_type=jnp.float32)
    )
    grad_norm_in, grad_first_gain, grad_first_shift = norm_backward(
        grad_normed, normal_first, inverse_first, first_gain
    )
    grad_inputs = grad_middle + grad_norm_in
    dense_sums = (
        lax.psum_scatter(grad_first_gain, ("rep", "exp"), scatter_dimension=0, tiled=True),
        lax.psum_scatter(grad_first_shift, ("rep", "exp"), scatter_dimension=0, tiled=True),
        lax.psum_scatter(grad_w_query, ("rep", "exp"), scatter_dimension=0, tiled=True),
        lax.psum_scatter(grad_w_key, ("rep", "exp"), scatter_dimension=0, tiled=True),
        lax.psum_scatter(grad_w_value, ("rep", "exp"), scatter_dimension=0, tiled=True),
        lax.psum_scatter(grad_w_output, ("rep", "exp"), scatter_dimension=0, tiled=True),
        lax.psum_scatter(grad_second_gain, ("rep", "exp"), scatter_dimension=0, tiled=True),
        lax.psum_scatter(grad_second_shift, ("rep", "exp"), scatter_dimension=0, tiled=True),
    )
    return (
        outputs.reshape(seq_count, seq_len, width),
        grad_inputs.reshape(seq_count, seq_len, width),
        dense_sums[0],
        dense_sums[1],
        dense_sums[2],
        dense_sums[3],
        dense_sums[4],
        dense_sums[5],
        dense_sums[6],
        dense_sums[7],
        grad_expert_in,
        grad_expert_out,
    )


def solution(mesh):
    placed = (
        P(("rep", "exp"), None, None),
        P(("rep", "exp"), None, None),
        P(("rep", "exp"), None),
        P(("rep", "exp")),
        P(),
        P(),
        P(),
        P(),
        P(),
        P(),
        P(),
        P(),
        P(),
        P("exp", None, None),
        P("exp", None, None),
    )
    return jax.shard_map(
        body,
        mesh=mesh,
        in_specs=placed,
        out_specs=(
            P(("rep", "exp"), None, None),
            P(("rep", "exp"), None, None),
            P(("rep", "exp")),
            P(("rep", "exp")),
            P(("rep", "exp"), None),
            P(("rep", "exp"), None),
            P(("rep", "exp"), None),
            P(("rep", "exp"), None),
            P(("rep", "exp")),
            P(("rep", "exp")),
            P("exp", "rep", None),
            P("exp", "rep", None),
        ),
        check_vma=False,
    )
```

profile of v0, /device:TPU:0, one launch (start us, length us, event | category | flops | bytes accessed | tf_op | source)
XLA Modules:
  0.0 1134.8 jit_solution(14569271297392837682)
XLA Ops:
  36.3 14.2 %fusion.3 = (f32[16,512]{1,0:T(8,128)S(1)}, f32[16,512,1024]{2,1,0:T(8,128)}) fusion(pred[512,1024]{1,0:T(8,128)(4,1)S(1)} %get-tuple-element.121, bf16[512,16,64]{0,2,1:T(8,128)(2,1)S(1)} %bitcast.180, bf16[1024,16,64]{0,2,1:T(8,128)(2,1)S(1)} %bitcast.176), kind=kOutput, calls=%fused_computation.22 | convolution fusion | flops 1098899456 | bytes 37257216 | tf_op jit(solution)/shard_map/while/body/eval_jaxpr/qhd,khd->hqk/dot_general | solution.py:47
  50.4 14.9 %fusion.1 = f32[16,512]{1,0:T(8,128)S(1)} fusion(f32[16,512,1024]{2,1,0:T(8,128)} %get-tuple-element.123, f32[16,512]{1,0:T(8,128)S(1)} %get-tuple-element.122, pred[512,1024]{1,0:T(8,128)(4,1)S(1)} %get-tuple-element.121), kind=kLoop, calls=%fused_computation.18 | loop fusion | flops 33546240 | bytes 34144256 | tf_op jit(solution)/shard_map/while/body/eval_jaxpr/reduce_sum | solution.py:68
  65.4 14.4 %fusion.75 = bf16[16,64,512]{2,1,0:T(8,128)(2,1)S(1)} fusion(bf16[1024,16,64]{0,2,1:T(8,128)(2,1)S(1)} %bitcast.205, f32[16,512,1024]{2,1,0:T(8,128)} %get-tuple-element.123, f32[16,512]{1,0:T(8,128)S(1)} %fusion.1, f32[16,512]{1,0:T(8,128)S(1)} %get-tuple-element.122, pred[512,1024]{1,0:T(8,128)(4,1)S(1)} %get-tuple-element.121), kind=kOutput, calls=%fused_computation.124 | convolution fusion | flops 1116209152 | bytes 37289984 | tf_op jit(solution)/shard_map/while/body/eval_jaxpr/hqk,khd->qhd/dot_general | solution.py:71
  79.9 13.9 %fusion.2 = (f32[16,512]{1,0:T(8,128)S(1)}, f32[16,512,1024]{2,1,0:T(8,128)}) fusion(pred[512,1024]{1,0:T(8,128)(4,1)S(1)} %get-tuple-element.120, bf16[512,16,64]{0,2,1:T(8,128)(2,1)S(1)} %bitcast.182, bf16[1024,16,64]{0,2,1:T(8,128)(2,1)S(1)} %bitcast.177), kind=kOutput, calls=%fused_computation.21 | convolution fusion | flops 1098899456 | bytes 37257216 | tf_op jit(solution)/shard_map/while/body/eval_jaxpr/qhd,khd->hqk/dot_general | solution.py:47
  93.7 14.9 %fusion = f32[16,512]{1,0:T(8,128)S(1)} fusion(f32[16,512,1024]{2,1,0:T(8,128)} %get-tuple-element.125, f32[16,512]{1,0:T(8,128)S(1)} %get-tuple-element.124, pred[512,1024]{1,0:T(8,128)(4,1)S(1)} %get-tuple-element.120), kind=kLoop, calls=%fused_computation.17 | loop fusion | flops 33546240 | bytes 34144256 | tf_op jit(solution)/shard_map/while/body/eval_jaxpr/reduce_sum | solution.py:68
  108.7 24.9 %fusion.76 = bf16[16,64,512]{2,1,0:T(8,128)(2,1)S(1)} fusion(bf16[1024,16,64]{0,2,1:T(8,128)(2,1)S(1)} %bitcast.206, f32[16,512,1024]{2,1,0:T(8,128)} %get-tuple-element.125, f32[16,512]{1,0:T(8,128)S(1)} %fusion, f32[16,512]{1,0:T(8,128)S(1)} %get-tuple-element.124, pred[512,1024]{1,0:T(8,128)(4,1)S(1)} %get-tuple-element.120), kind=kOutput, calls=%fused_computation.125 | convolution fusion | flops 1116209152 | bytes 37289984 | tf_op jit(solution)/shard_map/while/body/eval_jaxpr/hqk,khd->qhd/dot_general | solution.py:71
  177.1 7.9 all-to-all-done
  189.4 47.8 %fusion.6 = (bf16[1024,4096]{1,0:T(8,128)(2,1)}, f32[1024,4096]{1,0:T(8,128)}) fusion(bf16[1024,1024]{1,0:T(8,128)(2,1)} %bitcast.17, bf16[1,4096,1024]{2,1,0:T(8,128)(2,1)} %param.28), kind=kOutput, calls=%fused_computation.25 | convolution fusion | flops 8862564352 | bytes 35651584 | tf_op jit(solution)/shard_map/rd,fd->rf/dot_general | solution.py:179
  237.1 16.8 %fusion.12 = bf16[1024,4096]{1,0:T(8,128)(2,1)S(1)} fusion(f32[1024,4096]{1,0:T(8,128)} %get-tuple-element.129, bf16[1024,1024]{1,0:T(8,128)(2,1)} %bitcast.25, bf16[1,4096,1024]{2,1,0:T(8,128)(2,1)} %param.29), kind=kOutput, calls=%fused_computation.31 | convolution fusion | flops 8631877632 | bytes 35651584 | tf_op jit(solution)/shard_map/re,fe->rf/dot_general | solution.py:199
  257.2 12.9 %convert_bitcast_fusion.1 = bf16[1,4096,1024]{2,1,0:T(8,128)(2,1)} fusion(bf16[1024,4096]{1,0:T(8,128)(2,1)S(1)} %fusion.12, bf16[1024,1024]{1,0:T(8,128)(2,1)} %bitcast.17), kind=kOutput, calls=%fused_computation.61 | convolution fusion | flops 8594128896 | bytes 18874368 | tf_op jit(solution)/shard_map/rf,rd->fd/dot_general | solution.py:203
  270.2 15.1 %convert_bitcast_fusion = bf16[1,4096,1024]{2,1,0:T(8,128)(2,1)} fusion(bf16[1024,4096]{1,0:T(8,128)(2,1)} %get-tuple-element.128, bf16[1024,1024]{1,0:T(8,128)(2,1)} %bitcast.25), kind=kOutput, calls=%fused_computation.60 | convolution fusion | flops 8594128896 | bytes 18874368 | tf_op jit(solution)/shard_map/rf,re->fe/dot_general | solution.py:204
  285.3 14.7 %fusion.69 = bf16[1024,1024]{1,0:T(8,128)(2,1)} fusion(bf16[1024,4096]{1,0:T(8,128)(2,1)} %copy-done.68, bf16[1,4096,1024]{2,1,0:T(8,128)(2,1)} %param.28), kind=kOutput, calls=%fused_computation.122 | convolution fusion | flops 8590983168 | bytes 18874368 | tf_op jit(solution)/shard_map/dot_general | solution.py:16
  304.4 14.8 %fusion.72 = bf16[1024,1024]{1,0:T(8,128)(2,1)} fusion(bf16[1024,4096]{1,0:T(8,128)(2,1)} %get-tuple-element.128, bf16[1,4096,1024]{2,1,0:T(8,128)(2,1)} %param.29), kind=kOutput, calls=%fused_computation.123 | convolution fusion | flops 8590983168 | bytes 18874368 | tf_op jit(solution)/shard_map/dot_general | solution.py:16
  319.2 11.8 %all-to-all-done.3 = bf16[8,128,1024]{2,1,0:T(8,128)(2,1)} async-done(((bf16[8,128,1024]{2,1,0:T(8,128)(2,1)}), bf16[8,128,1024]{2,1,0:T(8,128)(2,1)}, u32[]{:S(2)}, u32[]{:S(2)}) %all-to-all-start.3) | async-done | bytes 2097184 | tf_op jit(solution)/shard_map/all_to_all | solution.py:216
  335.6 8.1 gather_fusion.2
  347.6 14.5 %all-to-all-done.1 = bf16[8,128,1024]{2,1,0:T(8,128)(2,1)} async-done(((bf16[8,128,1024]{2,1,0:T(8,128)(2,1)}), bf16[8,128,1024]{2,1,0:T(8,128)(2,1)}, u32[]{:S(2)}, u32[]{:S(2)}) %all-to-all-start.1) | async-done | bytes 2097184 | tf_op jit(solution)/shard_map/all_to_all | solution.py:182
  362.1 7.9 gather_fusion.1
  394.1 17.9 %fusion.13 = f32[16,64,1024]{2,1,0:T(8,128)} fusion(bf16[512,16,64]{0,2,1:T(8,128)(2,1)} %bitcast.194, f32[16,512,1024]{2,1,0:T(8,128)} %get-tuple-element.123, f32[16,512]{1,0:T(8,128)S(1)} %log_add_fusion, pred[512,1024]{1,0:T(8,128)(4,1)S(1)} %copy-done.15), kind=kOutput, calls=%fused_computation.32 | convolution fusion | flops 1115684864 | bytes 39354368 | tf_op jit(solution)/shard_map/while/body/eval_jaxpr/hqk,qhd->khd/dot_general | solution.py:113
  412.0 18.4 %add_convert_fusion = bf16[16,64,1024]{2,1,0:T(8,128)(2,1)} fusion(f32[16,64,1024]{2,1,0:T(8,128)} %fusion.13, bf16[512,16,64]{0,2,1:T(8,128)(2,1)} %bitcast.196, f32[16,512]{1,0:T(8,128)S(1)} %log_add_fusion.1, f32[16,512,1024]{2,1,0:T(8,128)} %get-tuple-element.125, pred[512,1024]{1,0:T(8,128)(4,1)S(1)} %copy-done.18), kind=kOutput, calls=%fused_computation.99 | convolution fusion | flops 1117782016 | bytes 41451520 | tf_op jit(solution)/shard_map/while/body/eval_jaxpr/hqk,qhd->khd/dot_general | solution.py:113
  437.1 27.3 %multiply_reduce_fusion.1 = (f32[16,512]{1,0:T(8,128)S(1)}, f32[16,512,1024]{2,1,0:T(8,128)}) fusion(f32[16,512]{1,0:T(8,128)S(1)} %log_add_fusion.1, f32[16,512,1024]{2,1,0:T(8,128)} %get-tuple-element.125, pred[512,1024]{1,0:T(8,128)(4,1)S(1)} %copy-done.18, bf16[512,16,64]{0,2,1:T(8,128)(2,1)} %bitcast.197, bf16[1024,16,64]{0,2,1:T(8,128)(2,1)} %bitcast.207), kind=kOutput, calls=%fused_computation.9 | convolution fusion | flops 1124065280 | bytes 70844416 | tf_op jit(solution)/shard_map/while/body/eval_jaxpr/qhd,khd->hqk/dot_general | solution.py:99
  464.5 28.4 %multiply_convert_fusion.1 = bf16[16,512,1024]{2,1,0:T(8,128)(2,1)} fusion(f32[16,512,1024]{2,1,0:T(8,128)} %get-tuple-element.133, f32[16,512]{1,0:T(8,128)S(1)} %get-tuple-element.132, f32[16,512]{1,0:T(8,128)S(1)} %log_add_fusion.1, f32[16,512,1024]{2,1,0:T(8,128)} %get-tuple-element.125, pred[512,1024]{1,0:T(8,128)(4,1)} %copy-done.17), kind=kLoop, calls=%fused_computation.8 | loop fusion | flops 58720256 | bytes 84475904 | tf_op jit(solution)/shard_map/while/body/eval_jaxpr/convert_element_type | solution.py:103
  492.9 11.3 fusion.118
  504.2 26.5 %multiply_reduce_fusion = (f32[16,512]{1,0:T(8,128)S(1)}, f32[16,512,1024]{2,1,0:T(8,128)}) fusion(f32[16,512]{1,0:T(8,128)S(1)} %log_add_fusion, f32[16,512,1024]{2,1,0:T(8,128)} %get-tuple-element.123, pred[512,1024]{1,0:T(8,128)(4,1)S(1)} %copy-done.16, bf16[512,16,64]{0,2,1:T(8,128)(2,1)S(1)} %bitcast.195, bf16[1024,16,64]{0,2,1:T(8,128)(2,1)S(1)} %bitcast.208), kind=kOutput, calls=%fused_computation.6 | convolution fusion | flops 1124065280 | bytes 70844416 | tf_op jit(solution)/shard_map/while/body/eval_jaxpr/qhd,khd->hqk/dot_general | solution.py:99
  530.7 28.8 %multiply_convert_fusion = bf16[16,512,1024]{2,1,0:T(8,128)(2,1)} fusion(f32[16,512,1024]{2,1,0:T(8,128)} %get-tuple-element.131, f32[16,512]{1,0:T(8,128)S(1)} %get-tuple-element.130, f32[16,512]{1,0:T(8,128)S(1)} %log_add_fusion, f32[16,512,1024]{2,1,0:T(8,128)} %get-tuple-element.123, pred[512,1024]{1,0:T(8,128)(4,1)} %copy-done.14), kind=kLoop, calls=%fused_computation.5 | loop fusion | flops 58720256 | bytes 84475904 | tf_op jit(solution)/shard_map/while/body/eval_jaxpr/convert_element_type | solution.py:103
  559.5 10.2 multiply_convert_fusion.2
  575.5 11.6 %multiply_convert_fusion.4 = bf16[16,64,512]{2,1,0:T(8,128)(2,1)S(1)} fusion(bf16[1024,16,64]{0,2,1:T(8,128)(2,1)} %bitcast.178, bf16[16,512,1024]{2,1,0:T(8,128)(2,1)} %multiply_convert_fusion.1), kind=kOutput, calls=%fused_computation.112 | convolution fusion | flops 1074790400 | bytes 19922944 | tf_op jit(solution)/shard_map/while/body/eval_jaxpr/hqk,khd->qhd/dot_general | solution.py:105
  587.1 12.7 %multiply_convert_fusion.3 = bf16[16,64,512]{2,1,0:T(8,128)(2,1)} fusion(bf16[1024,16,64]{0,2,1:T(8,128)(2,1)} %bitcast.179, bf16[16,512,1024]{2,1,0:T(8,128)(2,1)} %multiply_convert_fusion), kind=kOutput, calls=%fused_computation.111 | convolution fusion | flops 1074790400 | bytes 19922944 | tf_op jit(solution)/shard_map/while/body/eval_jaxpr/hqk,khd->qhd/dot_general | solution.py:105
  622.3 40.5 %all-reduce.4 = (f32[1024]{0:T(1024)S(1)}, f32[1024]{0:T(1024)S(1)}, f32[1024]{0:T(1024)S(1)}, f32[1024]{0:T(1024)S(1)}) all-reduce(f32[1024]{0:T(1024)S(1)} %get-tuple-element.101, f32[1024]{0:T(1024)S(1)} %get-tuple-element.104, f32[1024]{0:T(1024)S(1)} %copy-done.44, ...), channel_id=2, replica_groups=mesh['rep'=4,'exp'=8] {'rep','exp'}, use_global_device_ids=true, to_apply=%region_20.21.clone | all-reduce | flops 4096 | bytes 32768
  686.1 22.9 %reduce-scatter.13.cloned.1.call-done = f32[32,1024]{1,0:T(8,128)} async-done(((f32[1024,1024]{1,0:T(8,128)}), f32[32,1024]{1,0:T(8,128)}) %reduce-scatter.13.cloned.1.call-update) | async-done | bytes 131088 | tf_op jit(solution)/shard_map/reduce_scatter | solution.py:260
  709.1 139.6 %reduce-scatter.11.cloned.1.call-done = f32[32,1024]{1,0:T(8,128)} async-done(((f32[1024,1024]{1,0:T(8,128)}), f32[32,1024]{1,0:T(8,128)}) %reduce-scatter.11.cloned.1.call-update) | async-done | bytes 131088 | tf_op jit(solution)/shard_map/reduce_scatter | solution.py:259
  848.6 139.4 %reduce-scatter.9.cloned.1.call-done = f32[32,1024]{1,0:T(8,128)} async-done(((f32[1024,1024]{1,0:T(8,128)}), f32[32,1024]{1,0:T(8,128)}) %reduce-scatter.9.cloned.1.call-update) | async-done | bytes 131088 | tf_op jit(solution)/shard_map/reduce_scatter | solution.py:258
  988.0 139.5 %reduce-scatter.7.cloned.1.call-done = f32[32,1024]{1,0:T(8,128)} async-done(((f32[1024,1024]{1,0:T(8,128)}), f32[32,1024]{1,0:T(8,128)}) %reduce-scatter.7.cloned.1.call-update) | async-done | bytes 131088 | tf_op jit(solution)/shard_map/reduce_scatter | solution.py:257
  (225 shorter events, 174.1 us)
Async XLA Ops:
  7.2 24.9 %copy-start = (bf16[1024,1024]{1,0:T(8,128)(2,1)S(1)}, bf16[1024,1024]{1,0:T(8,128)(2,1)}, u32[]{:S(2)}) copy-start(bf16[1024,1024]{1,0:T(8,128)(2,1)} %param.24) | copy-start | bytes 6291460
  15.1 19.6 %copy-start.34 = (s32[1024]{0:T(1024)}, s32[1024]{0:T(1024)S(1)}, u32[]{:S(2)}) copy-start(s32[1024]{0:T(1024)S(1)} %gather_fusion) | copy-start | bytes 12292
  29.1 50.7 %copy-start.1 = (bf16[1024,1024]{0,1:T(8,128)(2,1)}, bf16[1024,1024]{0,1:T(8,128)(2,1)S(1)}, u32[]{:S(2)}) copy-start(bf16[1024,1024]{0,1:T(8,128)(2,1)S(1)} %convolution_convert_fusion.1) | copy-start | bytes 6291460
  32.1 47.8 %copy-start.11 = (bf16[512,1024]{0,1:T(8,128)(2,1)}, bf16[512,1024]{0,1:T(8,128)(2,1)S(1)}, u32[]{:S(2)}) copy-start(bf16[512,1024]{0,1:T(8,128)(2,1)S(1)} %get-tuple-element.118) | copy-start | bytes 3145732
  34.8 73.9 %copy-start.61 = (bf16[1024,1024]{0,1:T(8,128)(2,1)}, bf16[1024,1024]{0,1:T(8,128)(2,1)S(1)}, u32[]{:S(2)}) copy-start(bf16[1024,1024]{0,1:T(8,128)(2,1)S(1)} %convolution_convert_fusion.3) | copy-start | bytes 6291460
  36.2 29.1 %copy-start.14 = (pred[512,1024]{1,0:T(8,128)(4,1)}, pred[512,1024]{1,0:T(8,128)(4,1)S(1)}, u32[]{:S(2)}) copy-start(pred[512,1024]{1,0:T(8,128)(4,1)S(1)} %get-tuple-element.121) | copy-start | bytes 1572868
  36.2 72.4 %copy-start.17 = (pred[512,1024]{1,0:T(8,128)(4,1)}, pred[512,1024]{1,0:T(8,128)(4,1)S(1)}, u32[]{:S(2)}) copy-start(pred[512,1024]{1,0:T(8,128)(4,1)S(1)} %get-tuple-element.120) | copy-start | bytes 1572868
  79.8 53.8 %copy-start.64 = (bf16[16,64,512]{2,1,0:T(8,128)(2,1)}, bf16[16,64,512]{2,1,0:T(8,128)(2,1)S(1)}, u32[]{:S(2)}) copy-start(bf16[16,64,512]{2,1,0:T(8,128)(2,1)S(1)} %fusion.75) | copy-start | bytes 3145732
  108.7 24.9 %copy-start.28 = (f32[16,512]{1,0:T(8,128)}, f32[16,512]{1,0:T(8,128)S(1)}, u32[]{:S(2)}) copy-start(f32[16,512]{1,0:T(8,128)S(1)} %fusion) | copy-start | bytes 98308
  108.7 24.9 %copy-start.5 = (bf16[1,1024,1024]{1,2,0:T(8,128)(2,1)S(1)}, bf16[1,1024,1024]{1,2,0:T(8,128)(2,1)}, u32[]{:S(2)}) copy-start(bf16[1,1024,1024]{1,2,0:T(8,128)(2,1)} %copy.49) | copy-start | bytes 6291460
  108.7 24.9 %copy-start.54 = (bf16[1024,1024]{1,0:T(8,128)(2,1)S(1)}, bf16[1024,1024]{1,0:T(8,128)(2,1)}, u32[]{:S(2)}) copy-start(bf16[1024,1024]{1,0:T(8,128)(2,1)} %param.25) | copy-start | bytes 6291460
  145.4 24.2 %copy-start.46 = (s32[1024,1]{0,1:T(1,128)}, s32[1024,1]{0,1:T(1,128)S(1)}, u32[]{:S(2)}) copy-start(s32[1024,1]{0,1:T(1,128)S(1)} %compare_select_fusion) | copy-start | bytes 12292
  152.9 32.1 %all-to-all-start = ((bf16[8,128,1024]{2,1,0:T(8,128)(2,1)}), bf16[8,128,1024]{2,1,0:T(8,128)(2,1)}, u32[]{:S(2)}, u32[]{:S(2)}) async-start(bf16[8,128,1024]{2,1,0:T(8,128)(2,1)} %bitcast.185), calls=%async_computation | async-start | bytes 4194304 | tf_op jit(solution)/shard_map/all_to_all | solution.py:174
  185.0 52.2 %all-to-all-start.2 = ((bf16[8,128,1024]{2,1,0:T(8,128)(2,1)}), bf16[8,128,1024]{2,1,0:T(8,128)(2,1)}, u32[]{:S(2)}, u32[]{:S(2)}) async-start(bf16[8,128,1024]{2,1,0:T(8,128)(2,1)} %bitcast.184), calls=%async_computation.2 | async-start | bytes 4194304 | tf_op jit(solution)/shard_map/all_to_all | solution.py:196
  189.3 488.6 %reduce-scatter.15.cloned.1.call-start = ((), (), s32[]{:S(2)}) async-start(), calls=%async_computation.14 | async-start | bytes 10485760 | tf_op jit(solution)/shard_map/reduce_scatter | solution.py:209
  270.1 411.9 %reduce-scatter.17.cloned.1.call-start = ((), (), s32[]{:S(2)}) async-start(), calls=%async_computation.15 | async-start | bytes 10485760 | tf_op jit(solution)/shard_map/reduce_scatter | solution.py:212
  300.0 31.0 %all-to-all-start.3 = ((bf16[8,128,1024]{2,1,0:T(8,128)(2,1)}), bf16[8,128,1024]{2,1,0:T(8,128)(2,1)}, u32[]{:S(2)}, u32[]{:S(2)}) async-start(bf16[8,128,1024]{2,1,0:T(8,128)(2,1)} %bitcast.189), calls=%async_computation.3 | async-start | bytes 4194304 | tf_op jit(solution)/shard_map/all_to_all | solution.py:216
  319.2 16.3 %copy-start.27 = (f32[16,512]{1,0:T(8,128)S(1)}, f32[16,512]{1,0:T(8,128)}, u32[]{:S(2)}) copy-start(f32[16,512]{1,0:T(8,128)} %copy-done.26) | copy-start | bytes 98308
  319.2 16.3 %copy-start.25 = (f32[16,512]{1,0:T(8,128)S(1)}, f32[16,512]{1,0:T(8,128)}, u32[]{:S(2)}) copy-start(f32[16,512]{1,0:T(8,128)} %copy-done.24) | copy-start | bytes 98308
  319.2 16.3 %copy-start.29 = (f32[16,512]{1,0:T(8,128)S(1)}, f32[16,512]{1,0:T(8,128)}, u32[]{:S(2)}) copy-start(f32[16,512]{1,0:T(8,128)} %copy-done.28) | copy-start | bytes 98308
  331.1 31.0 %all-to-all-start.1 = ((bf16[8,128,1024]{2,1,0:T(8,128)(2,1)}), bf16[8,128,1024]{2,1,0:T(8,128)(2,1)}, u32[]{:S(2)}, u32[]{:S(2)}) async-start(bf16[8,128,1024]{2,1,0:T(8,128)(2,1)} %bitcast.188), calls=%async_computation.1 | async-start | bytes 4194304 | tf_op jit(solution)/shard_map/all_to_all | solution.py:182
  335.4 373.6 %reduce-scatter.13.cloned.1.call-start = ((), (), s32[]{:S(2)}) async-start(), calls=%async_computation.13 | async-start | bytes 4325376 | tf_op jit(solution)/shard_map/reduce_scatter | solution.py:260
  393.0 455.6 %reduce-scatter.11.cloned.1.call-start = ((), (), s32[]{:S(2)}) async-start(), calls=%async_computation.12 | async-start | bytes 4325376 | tf_op jit(solution)/shard_map/reduce_scatter | solution.py:259
  394.1 17.9 %copy-start.18 = (pred[512,1024]{1,0:T(8,128)(4,1)S(1)}, pred[512,1024]{1,0:T(8,128)(4,1)}, u32[]{:S(2)}) copy-start(pred[512,1024]{1,0:T(8,128)(4,1)} %copy-done.17) | copy-start | bytes 1572868
  412.0 18.5 %copy-start.39 = (f32[1024]{0:T(1024)S(1)}, f32[1024]{0:T(1024)}, u32[]{:S(2)}) copy-start(f32[1024]{0:T(1024)} %copy-done.38) | copy-start | bytes 12292
  412.0 18.5 %copy-start.43 = (f32[1024]{0:T(1024)S(1)}, f32[1024]{0:T(1024)}, u32[]{:S(2)}) copy-start(f32[1024]{0:T(1024)} %copy-done.42) | copy-start | bytes 12292
  412.0 18.5 %copy-start.53 = (f32[1024]{0:T(1024)S(1)}, f32[1024]{0:T(1024)}, u32[]{:S(2)}) copy-start(f32[1024]{0:T(1024)} %param.20) | copy-start | bytes 12292
  412.0 18.5 %copy-start.60 = (f32[1024]{0:T(1024)S(1)}, f32[1024]{0:T(1024)}, u32[]{:S(2)}) copy-start(f32[1024]{0:T(1024)} %param.21) | copy-start | bytes 12292
  464.4 523.6 %reduce-scatter.9.cloned.1.call-start = ((), (), s32[]{:S(2)}) async-start(), calls=%async_computation.11 | async-start | bytes 4325376 | tf_op jit(solution)/shard_map/reduce_scatter | solution.py:258
  464.5 28.4 %copy-start.12 = (bf16[512,1024]{0,1:T(8,128)(2,1)S(1)}, bf16[512,1024]{0,1:T(8,128)(2,1)}, u32[]{:S(2)}) copy-start(bf16[512,1024]{0,1:T(8,128)(2,1)} %copy-done.11) | copy-start | bytes 3145732
  530.7 28.8 %copy-start.9 = (bf16[512,1024]{0,1:T(8,128)(2,1)S(1)}, bf16[512,1024]{0,1:T(8,128)(2,1)}, u32[]{:S(2)}) copy-start(bf16[512,1024]{0,1:T(8,128)(2,1)} %copy-done.8) | copy-start | bytes 3145732
  575.5 552.0 %reduce-scatter.7.cloned.1.call-start = ((), (), s32[]{:S(2)}) async-start(), calls=%async_computation.10 | async-start | bytes 4325376 | tf_op jit(solution)/shard_map/reduce_scatter | solution.py:257
  (48 other events, 291.8 us)
Sparse Core Ops, SparseCore 0:
  270.3 146.5 reduce-scatter.14
  419.2 145.1 reduce-scatter.16
  567.3 141.6 reduce-scatter.12
  711.8 136.8 reduce-scatter.10
  851.3 136.6 reduce-scatter.8
  990.7 136.7 reduce-scatter.6
where the time goes:
time: 1140 us; the launch traced here: 1130 us
  waiting for transfers between devices  476 us (42%)
  matrix products  372 us (33%)
  other arithmetic  129 us (11%)
  local copies, waits for them, and re-layouts  82.9 us (7%)
  blocking collectives  40.5 us (4%)
  starting transfers between devices  18.6 us (2%)
  between operations  16.3 us (1%)
    reduce_scatter x1, waiting for transfers between devices, body(): lax.psum_scatter(grad_w_value, ('rep', 'exp'), scatter_dimension=0, tiled...  140 us
    reduce_scatter x1, waiting for transfers between devices, body(): lax.psum_scatter(grad_w_query, ('rep', 'exp'), scatter_dimension=0, tiled...  139 us
    reduce_scatter x1, waiting for transfers between devices, body(): lax.psum_scatter(grad_w_key, ('rep', 'exp'), scatter_dimension=0, tiled=T...  139 us
    convert_element_type x2, other arithmetic, attend_backward(): grad_scores = (shares * (grad_shares - row_delta)).astype(jnp.bfloat16)  57.1 us
    dot_general x2, matrix products, attend_backward(): jnp.einsum('qhd,khd->hqk', grad_blk, value_rows, preferred_element_type=j...  53.8 us
    dot_general x1, matrix products, body(): jnp.einsum('rd,fd->rf', arrived, weight_in, preferred_element_type=jnp.fl...  47.8 us
    unnamed x1, blocking collectives  40.5 us
    dot_general x6, matrix products, dot_float(): return jnp.dot(left, right, preferred_element_type=jnp.float32)  40.4 us
  transfers between devices with their start and end apart: 10, of which 7 were waited for; matrix products, arithmetic and copies ran while one was open for 36% of the time, Pallas kernels for 0%

commit v1 on v0

v1 whole, which is shorter than its diff:
```python
import functools
import math

import jax
import jax.numpy as jnp
from jax import lax
from jax.experimental import pallas as pl
from jax.experimental.pallas import tpu as pltpu
from jax.sharding import PartitionSpec as P

HEAD_DIM = 64
PAIR = 2 * HEAD_DIM
MASKED = -1e30
epsilon = 1e-05
bf16, f32 = jnp.bfloat16, jnp.float32
VMEM_BYTES = 56 * 1024 * 1024


def params():
    return pltpu.CompilerParams(vmem_limit_bytes=VMEM_BYTES)


def shape(dims, kind):
    return jax.ShapeDtypeStruct(dims, kind)


def nn(left, right):
    return lax.dot_general(left, right, (((1,), (0,)), ((), ())), preferred_element_type=f32)


def nt(left, right):
    return lax.dot_general(left, right, (((1,), (1,)), ((), ())), preferred_element_type=f32)


def tn(left, right):
    return lax.dot_general(left, right, (((0,), (0,)), ((), ())), preferred_element_type=f32)


def whole(array):
    return pl.BlockSpec(array.shape, lambda *_: (0,) * array.ndim)


def row_spec(rows, width):
    return pl.BlockSpec((rows, width), lambda i: (i, 0))


def normalize(values):
    average = jnp.mean(values, axis=1, keepdims=True)
    centered = values - average
    spread = jnp.mean(centered * centered, axis=1, keepdims=True)
    inverse = lax.rsqrt(spread + epsilon)
    return centered * inverse, inverse


def norm_backward(grad_out, normal, inverse, gain):
    grad_normal = grad_out * gain
    inner = (
        grad_normal
        - jnp.mean(grad_normal, axis=1, keepdims=True)
        - normal * jnp.mean(grad_normal * normal, axis=1, keepdims=True)
    )
    return inner * inverse


def gelu_parts(hidden):
    share = 0.5 * (1.0 + lax.erf(hidden * (1.0 / math.sqrt(2.0))))
    slope = share + hidden * jnp.exp(-0.5 * hidden * hidden) * (1.0 / math.sqrt(2.0 * math.pi))
    return hidden * share, slope


def route_kernel(len_ref, ids_ref, table_ref, cot_ref, place_ref, send_ref, *, groups, capacity):
    seq_len = ids_ref.shape[1]
    slot_total = groups * capacity
    high_count, low_count = table_ref.shape
    ids = ids_ref[...]
    high, low = ids // low_count, ids % low_count
    high_pick = (
        lax.broadcasted_iota(jnp.int32, (high_count, seq_len), 0) == high
    ).astype(f32).astype(bf16)
    picked = tn(table_ref[...].astype(bf16), high_pick)
    low_pick = lax.broadcasted_iota(jnp.int32, (low_count, seq_len), 0) == low
    expert = jnp.sum(jnp.where(low_pick, picked, 0.0), axis=0, keepdims=True)
    valid = lax.broadcasted_iota(jnp.int32, (1, seq_len), 1) < len_ref[0]
    own = lax.broadcasted_iota(jnp.int32, (groups, seq_len), 0).astype(f32)
    chosen = jnp.where((own == expert) & valid, 1.0, 0.0)
    earlier = (
        lax.broadcasted_iota(jnp.int32, (seq_len, seq_len), 0)
        < lax.broadcasted_iota(jnp.int32, (seq_len, seq_len), 1)
    ).astype(f32).astype(bf16)
    before = nn(chosen.astype(bf16), earlier)
    slot = jnp.sum(before * chosen, axis=0, keepdims=True)
    place = jnp.where(valid & (slot < capacity), expert * capacity + slot, float(slot_total))
    place_ref[...] = jnp.broadcast_to(place, place_ref.shape)
    send_ref[...] = nn(slot_pick(place, slot_total), cot_ref[...]).astype(bf16)


def slot_pick(place_row, slot_total):
    slots = lax.broadcasted_iota(jnp.int32, (slot_total, place_row.shape[1]), 0).astype(f32)
    return jnp.where(slots == place_row, 1.0, 0.0).astype(bf16)


def row_pick(place_rows, slot_total):
    column = place_rows.T[:, :1]
    slots = lax.broadcasted_iota(jnp.int32, (column.shape[0], slot_total), 1).astype(f32)
    return jnp.where(slots == column, 1.0, 0.0).astype(bf16)


def route(lengths, ids, table, cotangent, groups, capacity):
    rows, width = cotangent.shape
    return pl.pallas_call(
        functools.partial(route_kernel, groups=groups, capacity=capacity),
        in_specs=[
            pl.BlockSpec(memory_space=pltpu.SMEM),
            whole(ids),
            whole(table),
            whole(cotangent),
        ],
        out_specs=[
            pl.BlockSpec((8, rows), lambda: (0, 0)),
            pl.BlockSpec((groups * capacity, width), lambda: (0, 0)),
        ],
        out_shape=[shape((8, rows), f32), shape((groups * capacity, width), bf16)],
        compiler_params=params(),
    )(lengths, ids, table, cotangent)


def project_kernel(x_ref, gain_ref, shift_ref, wq_ref, wk_ref, wv_ref, n_ref, q_ref, k_ref, v_ref):
    normal, _ = normalize(x_ref[...].astype(f32))
    normed = (normal * gain_ref[...] + shift_ref[...]).astype(bf16)
    n_ref[...] = normed
    q_ref[...] = nn(normed, wq_ref[...]).astype(bf16)
    k_ref[...] = nn(normed, wk_ref[...]).astype(bf16)
    v_ref[...] = nn(normed, wv_ref[...]).astype(bf16)


def project(x, gain, shift, wq, wk, wv, block=256):
    rows, width = x.shape
    return pl.pallas_call(
        project_kernel,
        grid=(rows // block,),
        in_specs=[row_spec(block, width)] + [whole(a) for a in (gain, shift, wq, wk, wv)],
        out_specs=[row_spec(block, width)] * 4,
        out_shape=[shape((rows, width), bf16)] * 4,
        compiler_params=params(),
    )(x, gain, shift, wq, wk, wv)


def head_parts(length, block, seq_len):
    lane = lax.broadcasted_iota(jnp.int32, (1, PAIR), 1)
    position = lax.broadcasted_iota(jnp.int32, (seq_len, 1), 0)
    bias = jnp.where(position < length, 0.0, MASKED).astype(bf16)
    down = lax.broadcasted_iota(jnp.int32, (block, block), 0)
    across = lax.broadcasted_iota(jnp.int32, (block, block), 1)
    return lane // HEAD_DIM, lane % HEAD_DIM == 0, bias, down <= across


def attend_kernel(len_ref, q_ref, k_ref, v_ref, o_ref, log_ref, *, block, pairs):
    seq_len = q_ref.shape[0]
    factor = HEAD_DIM**-0.5 * math.log2(math.e)
    half, first_lane, bias, causal = head_parts(len_ref[0], block, seq_len)
    zero = jnp.zeros_like(bias)
    keys, queries, values = [], [], []
    for pair in range(pairs):
        lanes = slice(pair * PAIR, (pair + 1) * PAIR)
        q, k = q_ref[:, lanes], k_ref[:, lanes]
        value_t = v_ref[:, lanes].T
        for h in range(2):
            spare = jnp.where(first_lane & (half != h), 1.0, 0.0).astype(bf16)
            keys.append(jnp.where(half == h, k, bias * spare))
            queries.append(jnp.where(half == h, q, spare))
            values.append(
                jnp.concatenate(
                    [value_t[h * HEAD_DIM : (h + 1) * HEAD_DIM], jnp.ones((16, seq_len), bf16)],
                    axis=0,
                )
            )
    order = [(h, j) for j in range(seq_len // block) for h in range(2 * pairs)]

    def score(h, j):
        end = (j + 1) * block
        return nt(keys[h][:end], queries[h][j * block : end])

    def soften(scores, j):
        last = jnp.where(causal, scores[j * block :], MASKED)
        scores = last if j == 0 else jnp.concatenate([scores[: j * block], last], axis=0)
        highest = jnp.max(scores, axis=0, keepdims=True) * factor
        return jnp.exp2(scores * factor - highest).astype(bf16), highest

    def finish(powers, highest, h, j):
        rows = slice(j * block, (j + 1) * block)
        total = nn(values[h][:, : (j + 1) * block], powers)
        summed = total[HEAD_DIM : HEAD_DIM + 1]
        mixed = total[:HEAD_DIM] * (1.0 / summed)
        o_ref[rows, h * HEAD_DIM : (h + 1) * HEAD_DIM] = mixed.T.astype(bf16)
        log_ref[h // 2, h % 2 : h % 2 + 1, rows] = highest + jnp.log2(summed)

    ahead = score(*order[0])
    behind = None
    for step, (h, j) in enumerate(order):
        scores = ahead
        if step + 1 < len(order):
            ahead = score(*order[step + 1])
        if behind is not None:
            finish(*behind, *order[step - 1])
        behind = soften(scores, j)
    finish(*behind, *order[-1])


def attend(lengths, q, k, v, block=256, pairs=2):
    rows, width = q.shape
    lanes = pl.BlockSpec((rows, pairs * PAIR), lambda i: (0, i))
    return pl.pallas_call(
        functools.partial(attend_kernel, block=block, pairs=pairs),
        grid=(width // (pairs * PAIR),),
        in_specs=[pl.BlockSpec(memory_space=pltpu.SMEM)] + [lanes] * 3,
        out_specs=[lanes, pl.BlockSpec((pairs, 2, rows), lambda i: (i, 0, 0))],
        out_shape=[shape((rows, width), bf16), shape((width // PAIR, 2, rows), f32)],
        compiler_params=params(),
    )(lengths, q, k, v)


def attend_back_kernel(
    len_ref, q_ref, k_ref, v_ref, o_ref, g_ref, log_ref, dq_ref, dk_ref, dv_ref, *, block, pairs
):
    seq_len = q_ref.shape[0]
    blocks = seq_len // block
    scale = HEAD_DIM**-0.5
    factor = scale * math.log2(math.e)
    half, first_lane, bias, causal = head_parts(len_ref[0], block, seq_len)
    zero = jnp.zeros_like(bias)
    keys, queries, values, keys_t, logs, deltas = [], [], [], [], [], []
    for pair in range(pairs):
        lanes = slice(pair * PAIR, (pair + 1) * PAIR)
        q, k, v = q_ref[:, lanes], k_ref[:, lanes], v_ref[:, lanes]
        key_t = k.T
        product = (g_ref[:, lanes].astype(f32) * o_ref[:, lanes].astype(f32)).T
        for h in range(2):
            rows = slice(h * HEAD_DIM, (h + 1) * HEAD_DIM)
            spare = jnp.where(first_lane & (half != h), 1.0, 0.0).astype(bf16)
            keys.append(jnp.where(half == h, k, bias * spare))
            queries.append(jnp.where(half == h, q, spare))
            values.append(jnp.where(half == h, v, zero))
            keys_t.append(key_t[rows])
            logs.append(log_ref[pair, h : h + 1, :])
            deltas.append(jnp.sum(product[rows], axis=0, keepdims=True))
    order = [(h, i) for i in range(blocks) for h in range(2 * pairs)]
    query_sums = [[None] * blocks for _ in range(2 * pairs)]
    kept = {}

    def lanes_of(h):
        return slice((h // 2) * PAIR, (h // 2 + 1) * PAIR)

    def products(h, i):
        rows = slice(i * block, (i + 1) * block)
        return (
            nt(keys[h][rows], queries[h][i * block :]),
            nt(values[h][rows], g_ref[i * block :, lanes_of(h)]),
        )

    def shares_of(scores, grad_shares, h, i):
        shares = jnp.exp2(scores * factor - logs[h][:, i * block :])
        first = jnp.where(causal, shares[:, :block], 0.0)
        if i + 1 < blocks:
            first = jnp.concatenate([first, shares[:, block:]], axis=1)
        grad_scores = first * (grad_shares - deltas[h][:, i * block :])
        return first.astype(bf16), grad_scores.astype(bf16)

    def finish(shares, grad_scores, h, i):
        rows, lanes = slice(i * block, (i + 1) * block), lanes_of(h)
        grad_v = nn(shares, g_ref[i * block :, lanes])
        grad_k = nn(grad_scores, q_ref[i * block :, lanes])
        part = nn(keys_t[h][:, rows], grad_scores)
        for j in range(i, blocks):
            term = part[:, (j - i) * block : (j - i + 1) * block]
            held = query_sums[h][j]
            query_sums[h][j] = term if held is None else held + term
        dq_ref[rows, h * HEAD_DIM : (h + 1) * HEAD_DIM] = (
            (query_sums[h][i] * scale).T.astype(bf16)
        )
        kept[h] = (grad_k, grad_v)
        if h % 2:
            other_k, other_v = kept[h - 1]
            dk_ref[rows, lanes] = (jnp.where(half == 0, other_k, grad_k) * scale).astype(bf16)
            dv_ref[rows, lanes] = jnp.where(half == 0, other_v, grad_v).astype(bf16)

    ahead = products(*order[0])
    behind = None
    for step, (h, i) in enumerate(order):
        now = ahead
        if step + 1 < len(order):
            ahead = products(*order[step + 1])
        if behind is not None:
            finish(*behind, *order[step - 1])
        behind = shares_of(*now, h, i)
    finish(*behind, *order[-1])


def attend_back(lengths, q, k, v, mixed, grad_mixed, logs, block=256, pairs=2):
    rows, width = q.shape
    lanes = pl.BlockSpec((rows, pairs * PAIR), lambda i: (0, i))
    return pl.pallas_call(
        functools.partial(attend_back_kernel, block=block, pairs=pairs),
        grid=(width // (pairs * PAIR),),
        in_specs=[pl.BlockSpec(memory_space=pltpu.SMEM)]
        + [lanes] * 5
        + [pl.BlockSpec((pairs, 2, rows), lambda i: (i, 0, 0))],
        out_specs=[lanes] * 3,
        out_shape=[shape((rows, width), bf16)] * 3,
        compiler_params=params(),
    )(lengths, q, k, v, mixed, grad_mixed, logs)


def middle_kernel(x_ref, m_ref, w_ref, gain_ref, shift_ref, place_ref, mid_ref, send_ref, sent):
    step = pl.program_id(0)
    block = x_ref.shape[0]
    middle = x_ref[...].astype(f32) + nn(m_ref[...], w_ref[...])
    mid_ref[...] = middle
    normal, _ = normalize(middle)
    sent[pl.ds(step * block, block)] = (normal * gain_ref[...] + shift_ref[...]).astype(bf16)

    @pl.when(step == pl.num_programs(0) - 1)
    def _():
        pick = slot_pick(place_ref[:1], send_ref.shape[0])
        send_ref[...] = nn(pick, sent[...]).astype(bf16)


def middle_and_send(x, mixed, w_output, gain, shift, place, slot_total, block=256):
    rows, width = x.shape
    blocked = row_spec(block, width)
    return pl.pallas_call(
        middle_kernel,
        grid=(rows // block,),
        in_specs=[blocked, blocked] + [whole(a) for a in (w_output, gain, shift, place)],
        out_specs=[blocked, pl.BlockSpec((slot_total, width), lambda i: (0, 0))],
        out_shape=[shape((rows, width), f32), shape((slot_total, width), bf16)],
        scratch_shapes=[pltpu.VMEM((rows, width), bf16)],
        compiler_params=params(),
    )(x, mixed, w_output, gain, shift, place)


def expert_kernel(x_ref, g_ref, in_ref, out_ref, slots_ref, act_ref, total, *, chunk):
    step = pl.program_id(0)
    count = x_ref.shape[0] // chunk

    @pl.when(step == 0)
    def _():
        total[...] = jnp.zeros_like(total)

    def rows(r):
        return slice(r * chunk, (r + 1) * chunk)

    def first(r):
        return nt(x_ref[rows(r)], in_ref[...]), nt(g_ref[rows(r)], out_ref[...])

    def second(hidden, grad_activated, r):
        activated, slope = gelu_parts(hidden)
        act_ref[rows(r)] = activated.astype(bf16)
        return (grad_activated * slope).astype(bf16)

    def third(grad_hidden, r):
        total[rows(r)] += nn(grad_hidden, in_ref[...])

    ahead, behind = first(0), None
    for r in range(count):
        now = ahead
        if r + 1 < count:
            ahead = first(r + 1)
        if behind is not None:
            third(behind, r - 1)
        behind = second(*now, r)
    third(behind, count - 1)

    @pl.when(step == pl.num_programs(0) - 1)
    def _():
        slots_ref[...] = total[...].astype(bf16)


def expert_main(x, g, w_in, w_out, block=1024, chunk=256):
    rows, width = x.shape
    units = w_in.shape[0]
    return pl.pallas_call(
        functools.partial(expert_kernel, chunk=chunk),
        grid=(units // block,),
        in_specs=[whole(x), whole(g), row_spec(block, width), row_spec(block, width)],
        out_specs=[whole(x), pl.BlockSpec((rows, block), lambda i: (0, i))],
        out_shape=[shape((rows, width), bf16), shape((rows, units), bf16)],
        scratch_shapes=[pltpu.VMEM((rows, width), f32)],
        compiler_params=params(),
    )(x, g, w_in, w_out)


def result_kernel(a_ref, w_ref, o_ref):
    o_ref[...] = nn(a_ref[...], w_ref[...]).astype(bf16)


def expert_result(activated, w_out, block=256):
    rows, units = activated.shape
    width = w_out.shape[1]
    return pl.pallas_call(
        result_kernel,
        grid=(rows // block,),
        in_specs=[row_spec(block, units), whole(w_out)],
        out_specs=row_spec(block, width),
        out_shape=shape((rows, width), bf16),
        compiler_params=params(),
    )(activated, w_out)


def expert_grad_kernel(*refs, count, sub):
    x_refs, g_refs = refs[:count], refs[count : 2 * count]
    in_ref, out_ref, gin_ref, gout_ref = refs[2 * count :]
    order = [(r, p) for r in range(in_ref.shape[0] // sub) for p in range(count)]
    sums = [None]

    def rows(r):
        return slice(r * sub, (r + 1) * sub)

    def first(r, p):
        return nt(in_ref[rows(r)], x_refs[p][...]), nt(out_ref[rows(r)], g_refs[p][...])

    def second(hidden, grad_activated):
        activated, slope = gelu_parts(hidden)
        return activated.astype(bf16), (grad_activated * slope).astype(bf16)

    def third(activated, grad_hidden, r, p):
        grad_out = nn(activated, g_refs[p][...])
        grad_in = nn(grad_hidden, x_refs[p][...])
        if p:
            grad_out += gout_ref[rows(r)]
            grad_in += gin_ref[rows(r)]
        gout_ref[rows(r)] = grad_out
        gin_ref[rows(r)] = grad_in

    ahead, behind = first(*order[0]), None
    for step in range(len(order)):
        now = ahead
        if step + 1 < len(order):
            ahead = first(*order[step + 1])
        if behind is not None:
            third(*behind, *order[step - 1])
        behind = second(*now)
    third(*behind, *order[-1])


def expert_grads(xs, gs, w_in, w_out, block=256, sub=256):
    units, width = w_in.shape
    blocked = row_spec(block, width)
    return pl.pallas_call(
        functools.partial(expert_grad_kernel, count=len(xs), sub=sub),
        grid=(units // block,),
        in_specs=[whole(a) for a in (*xs, *gs)] + [blocked, blocked],
        out_specs=[blocked, blocked],
        out_shape=[shape((units, width), f32)] * 2,
        compiler_params=params(),
    )(*xs, *gs, w_in, w_out)


def back_kernel(
    back_ref, place_ref, mid_ref, cot_ref, len_ref, gain_ref, w_ref,
    gmid_ref, branch_ref, gmix_ref, ggain_ref, gshift_ref,
):
    step = pl.program_id(0)
    block = mid_ref.shape[0]
    grad_sent = nn(row_pick(place_ref[...], back_ref.shape[0]), back_ref[...])
    normal, inverse = normalize(mid_ref[...])
    position = step * block + lax.broadcasted_iota(jnp.int32, (block, 1), 0)
    grad_final = jnp.where(position < len_ref[0], cot_ref[...].astype(f32), 0.0)
    grad_middle = grad_final + norm_backward(grad_sent, normal, inverse, gain_ref[...])
    gmid_ref[...] = grad_middle
    branch = grad_middle.astype(bf16)
    branch_ref[...] = branch
    gmix_ref[...] = nt(branch, w_ref[...]).astype(bf16)

    @pl.when(step == 0)
    def _():
        ggain_ref[...] = jnp.zeros_like(ggain_ref)
        gshift_ref[...] = jnp.zeros_like(gshift_ref)

    ggain_ref[...] += jnp.sum(grad_sent * normal, axis=0, keepdims=True)
    gshift_ref[...] += jnp.sum(grad_sent, axis=0, keepdims=True)


def middle_back(back, place, middle, cotangent, lengths, gain, w_output, block=256):
    rows, width = middle.shape
    blocked = row_spec(block, width)
    vector = pl.BlockSpec((1, width), lambda i: (0, 0))
    return pl.pallas_call(
        back_kernel,
        grid=(rows // block,),
        in_specs=[
            whole(back),
            pl.BlockSpec((8, block), lambda i: (0, i)),
            blocked,
            blocked,
            pl.BlockSpec(memory_space=pltpu.SMEM),
            whole(gain),
            whole(w_output),
        ],
        out_specs=[blocked, blocked, blocked, vector, vector],
        out_shape=[shape((rows, width), f32)]
        + [shape((rows, width), bf16)] * 2
        + [shape((1, width), f32)] * 2,
        compiler_params=params(),
    )(back, place, middle, cotangent, lengths, gain, w_output)


def weight_grad_kernel(a_ref, *refs, kind):
    count = len(refs) // 2
    left = a_ref[...].T
    for b_ref, o_ref in zip(refs[:count], refs[count:]):
        o_ref[...] = nn(left, b_ref[...]).astype(kind)


def weight_grads(a, bs, block=256, kind=bf16):
    rows, width = a.shape
    out_width = bs[0].shape[1]
    return pl.pallas_call(
        functools.partial(weight_grad_kernel, kind=kind),
        grid=(width // block,),
        in_specs=[pl.BlockSpec((rows, block), lambda i: (0, i))] + [whole(b) for b in bs],
        out_specs=[row_spec(block, out_width)] * len(bs),
        out_shape=[shape((width, out_width), kind)] * len(bs),
        compiler_params=params(),
    )(a, *bs)


def input_back_kernel(
    gq_ref, gk_ref, gv_ref, wq_ref, wk_ref, wv_ref, x_ref, gmid_ref, gain_ref,
    gin_ref, ggain_ref, gshift_ref,
):
    grad_normed = (
        nt(gq_ref[...], wq_ref[...]) + nt(gk_ref[...], wk_ref[...]) + nt(gv_ref[...], wv_ref[...])
    )
    normal, inverse = normalize(x_ref[...].astype(f32))
    gin_ref[...] = gmid_ref[...] + norm_backward(grad_normed, normal, inverse, gain_ref[...])

    @pl.when(pl.program_id(0) == 0)
    def _():
        ggain_ref[...] = jnp.zeros_like(ggain_ref)
        gshift_ref[...] = jnp.zeros_like(gshift_ref)

    ggain_ref[...] += jnp.sum(grad_normed * normal, axis=0, keepdims=True)
    gshift_ref[...] += jnp.sum(grad_normed, axis=0, keepdims=True)


def input_back(gq, gk, gv, wq, wk, wv, x, grad_middle, gain, block=256):
    rows, width = x.shape
    blocked = row_spec(block, width)
    vector = pl.BlockSpec((1, width), lambda i: (0, 0))
    return pl.pallas_call(
        input_back_kernel,
        grid=(rows // block,),
        in_specs=[blocked] * 3 + [whole(w) for w in (wq, wk, wv)] + [blocked, blocked, whole(gain)],
        out_specs=[blocked, vector, vector],
        out_shape=[shape((rows, width), f32)] + [shape((1, width), f32)] * 2,
        compiler_params=params(),
    )(gq, gk, gv, wq, wk, wv, x, grad_middle, gain)


def output_kernel(back_ref, place_ref, mid_ref, o_ref):
    combined = nn(row_pick(place_ref[...], back_ref.shape[0]), back_ref[...])
    o_ref[...] = (mid_ref[...] + combined).astype(bf16)


def combine(back, place, middle, block=256):
    rows, width = middle.shape
    return pl.pallas_call(
        output_kernel,
        grid=(rows // block,),
        in_specs=[
            whole(back),
            pl.BlockSpec((8, block), lambda i: (0, i)),
            row_spec(block, width),
        ],
        out_specs=row_spec(block, width),
        out_shape=shape((rows, width), bf16),
        compiler_params=params(),
    )(back, place, middle)


def body(
    inputs,
    cotangent,
    token_ids,
    lengths,
    hash_table,
    first_gain,
    first_shift,
    w_query,
    w_key,
    w_value,
    w_output,
    second_gain,
    second_shift,
    expert_in,
    expert_out,
):
    seq_count, seq_len, width = inputs.shape
    rows = seq_count * seq_len
    groups = lax.axis_size("exp")
    copies = lax.axis_size("rep")
    place_z = lax.axis_index("rep")
    capacity = rows // groups
    slot_total = groups * capacity
    x = inputs.reshape(rows, width)
    cot = cotangent.reshape(rows, width)
    gain_one, shift_one, gain_two, shift_two = (
        v.reshape(1, width) for v in (first_gain, first_shift, second_gain, second_shift)
    )
    table_rows = -(-hash_table.shape[0] // (8 * 128)) * 8
    table = jnp.pad(hash_table, (0, table_rows * 128 - hash_table.shape[0]))
    table = table.reshape(table_rows, 128)

    def exchange(array):
        return lax.all_to_all(
            array.reshape(groups, capacity, width), "exp", split_axis=0, concat_axis=0, tiled=True
        ).reshape(slot_total, width)

    def spread(array):
        up, down = [array], [array]
        for _ in range(copies - 1):
            up.append(lax.ppermute(up[-1], "rep", [(i, i + 1) for i in range(copies - 1)]))
            down.append(lax.ppermute(down[-1], "rep", [(i + 1, i) for i in range(copies - 1)]))
        return [
            jnp.where(place_z >= step, up[step], down[copies - step]) for step in range(1, copies)
        ]

    place, grad_send = route(
        lengths, token_ids.reshape(1, rows), table, cot, groups, capacity
    )
    grad_arrived = exchange(grad_send)
    normed, q, k, v = project(x, gain_one, shift_one, w_query, w_key, w_value)
    mixed, logs = attend(lengths, q, k, v)
    middle, send_rows = middle_and_send(x, mixed, w_output, gain_two, shift_two, place, slot_total)
    arrived = exchange(send_rows)
    grad_slots, activated = expert_main(arrived, grad_arrived, expert_in[0], expert_out[0])
    grad_back = exchange(grad_slots)
    returned = exchange(expert_result(activated, expert_out[0]))
    grad_middle, branch, grad_mixed, grad_second_gain, grad_second_shift = middle_back(
        grad_back, place, middle, cot, lengths, gain_two, w_output
    )
    (grad_w_output,) = weight_grads(mixed, [branch])
    gq, gk, gv = attend_back(lengths, q, k, v, mixed, grad_mixed, logs)
    grad_qkv = weight_grads(normed, [gq, gk, gv])
    grad_inputs, grad_first_gain, grad_first_shift = input_back(
        gq, gk, gv, w_query, w_key, w_value, x, grad_middle, gain_one
    )
    outputs = combine(returned, place, middle)

    share = expert_in.shape[1] // copies
    shares = [
        lax.dynamic_slice_in_dim(w[0], place_z * share, share, axis=0)
        for w in (expert_in, expert_out)
    ]
    grad_expert_in, grad_expert_out = expert_grads(
        [arrived, *spread(arrived)], [grad_arrived, *spread(grad_arrived)], *shares
    )

    def scatter(arrays):
        devices = groups * copies
        parts = [a.reshape(copies, groups, width // devices, width) for a in arrays]
        joined = jnp.concatenate(parts, axis=2)
        joined = lax.psum_scatter(
            joined.transpose(1, 0, 2, 3), "exp", scatter_dimension=0, tiled=True
        )
        joined = lax.psum_scatter(joined[0], "rep", scatter_dimension=0, tiled=True)[0]
        return [part.astype(f32) for part in jnp.split(joined, len(arrays), axis=0)]

    (dense_output,) = scatter([grad_w_output])
    dense_query, dense_key, dense_value = scatter(grad_qkv)
    vectors = jnp.concatenate(
        [grad_first_gain, grad_first_shift, grad_second_gain, grad_second_shift], axis=0
    )
    vectors = lax.psum(vectors, ("rep", "exp"))
    part = width // (groups * copies)
    mine = (place_z * groups + lax.axis_index("exp")) * part
    vectors = lax.dynamic_slice_in_dim(vectors, mine, part, axis=1)
    return (
        outputs.reshape(seq_count, seq_len, width),
        grad_inputs.reshape(seq_count, seq_len, width),
        vectors[0],
        vectors[1],
        dense_query,
        dense_key,
        dense_value,
        dense_output,
        vectors[2],
        vectors[3],
        grad_expert_in[None],
        grad_expert_out[None],
    )


def solution(mesh):
    both = ("rep", "exp")
    placed = (
        P(both, None, None),
        P(both, None, None),
        P(both, None),
        P(both),
    ) + (P(),) * 9 + (P("exp", None, None),) * 2
    return jax.shard_map(
        body,
        mesh=mesh,
        in_specs=placed,
        out_specs=(
            P(both, None, None),
            P(both, None, None),
            P(both),
            P(both),
            P(both, None),
            P(both, None),
            P(both, None),
            P(both, None),
            P(both),
            P(both),
            P("exp", "rep", None),
            P("exp", "rep", None),
        ),
        check_vma=False,
    )
```

time: 1140 us -> 722 us (0.63)
  matrix products: 372 us -> 0 us
  waiting for transfers between devices: 476 us -> 224 us
  Pallas kernels: 0 us -> 220 us
  blocking collectives: 40.5 us -> 170 us
  other arithmetic: 129 us -> 29 us
  local copies, waits for them, and re-layouts: 82.9 us -> 14.3 us
  starting transfers between devices: 18.6 us -> 40.5 us
    reduce_scatter x6 -> x4, waiting for transfers between devices: 441 us -> 13.7 us  [the longest x2 13.7 us: scatter(): lax.psum_scatter(joined[0], 'rep', scatter_dimension=0, tiled=True)[0]]
    dot_general x30 -> x0, matrix products: 372 us -> none  [the longest x2 53.8 us: attend_backward(): jnp.einsum('qhd,khd->hqk', grad_blk, value_rows, preferred_element_type=j...]
    pallas_call x0 -> x13, Pallas kernels: none -> 220 us  [the longest x1 43 us: expert_grads(): pl.pallas_call(functools.partial(expert_grad_kernel, count=len(xs), sub=s...]
    ppermute x0 -> x12, waiting for transfers between devices: none -> 210 us  [the longest x6 141 us: spread(): lax.ppermute(down[-1], 'rep', [(i + 1, i) for i in range(copies - 1)])]
    all_to_all x0 -> x3, blocking collectives: none -> 92.9 us  [exchange(): lax.all_to_all(array.reshape(groups, capacity, width), 'exp', split_axis=...]
    psum x0 -> x1, blocking collectives: none -> 77.4 us  [body(): vectors = lax.psum(vectors, ('rep', 'exp'))]
    convert_element_type x7 -> x2, other arithmetic: 70.7 us -> 3.16 us  [scatter(): return [part.astype(f32) for part in jnp.split(joined, len(arrays), axis=0)]]
    unnamed x1 -> x0, blocking collectives: 40.5 us -> none
  transfers between devices with their start and end apart: 10 -> 17, of which waited for: 7 -> 7; matrix products, arithmetic and copies ran while one was open for 36% -> 5% of each run, Pallas kernels for 0% -> 17%
where the time goes in v1:
time: 722 us; the launch traced here: 713 us
  waiting for transfers between devices  224 us (31%)
  Pallas kernels  220 us (30%)
  blocking collectives  170 us (24%)
  starting transfers between devices  40.5 us (6%)
  other arithmetic  29 us (4%)
  between operations  15 us (2%)
  local copies, waits for them, and re-layouts  14.3 us (2%)
    ppermute x6, waiting for transfers between devices, spread(): lax.ppermute(down[-1], 'rep', [(i + 1, i) for i in range(copies - 1)])  141 us
    all_to_all x3, blocking collectives, exchange(): lax.all_to_all(array.reshape(groups, capacity, width), 'exp', split_axis=...  92.9 us
    psum x1, blocking collectives, body(): vectors = lax.psum(vectors, ('rep', 'exp'))  77.4 us
    ppermute x6, waiting for transfers between devices, spread(): lax.ppermute(up[-1], 'rep', [(i, i + 1) for i in range(copies - 1)])  69.7 us
    pallas_call x1, Pallas kernels, expert_grads(): pl.pallas_call(functools.partial(expert_grad_kernel, count=len(xs), sub=s...  43 us
    pallas_call x1, Pallas kernels, expert_main(): pl.pallas_call(functools.partial(expert_kernel, chunk=chunk), grid=(units...  33.6 us
    pallas_call x1, Pallas kernels, attend_back(): pl.pallas_call(functools.partial(attend_back_kernel, block=block, pairs=p...  31.1 us
    ppermute x6, starting transfers between devices, spread(): lax.ppermute(up[-1], 'rep', [(i, i + 1) for i in range(copies - 1)])  28.5 us
  transfers between devices with their start and end apart: 17, of which 7 were waited for; matrix products, arithmetic and copies ran while one was open for 5% of the time, Pallas kernels for 17%

profile of v1, /device:TPU:0, one launch (start us, length us, event | category | flops | bytes accessed | tf_op | source)
XLA Modules:
  0.0 713.0 jit_solution(18392035690549991577)
XLA Ops:
  9.2 12.3 %shard_map.238 = (bf16[1024,1024]{1,0:T(8,128)(2,1)}, bf16[1024,1024]{1,0:T(8,128)(2,1)}, bf16[1024,1024]{1,0:T(8,128)(2,1)}, bf16[1024,1024]{1,0:T(8,128)(2,1)}) custom-call(bf16[1024,1024]{1,0:T(8,128)(2,1)} %bitcast.65, f32[1,1024]{1,0:T(1,128)} %bitcast.95, f32[1,1024]{1,0:T(1,128)} %bitcast.97, bf16[1024,1024]{1,0:T(8,128)(2,1)} %wq_ref.3, ...), custom_call_target="tpu_custom_call" | custom-call | tf_op jit(solution)/shard_map/pallas_call | solution.py:138
  21.6 17.6 %shard_map.239 = (bf16[1024,1024]{1,0:T(8,128)(2,1)}, f32[8,2,1024]{2,1,0:T(2,128)}) custom-call(s32[1]{0:T(128)S(6)} %copy.35.len_ref, bf16[1024,1024]{1,0:T(8,128)(2,1)} %get-tuple-element.40.q_ref, bf16[1024,1024]{1,0:T(8,128)(2,1)} %get-tuple-element.41.k_ref, bf16[1024,1024]{1,0:T(8,128)(2,1)} %get-tuple-element.42.v_ref), custom_call_target="tpu_custom_call" | custom-call | tf_op jit(solution)/shard_map/pallas_call | solution.py:212
  39.2 5.7 shard_map.240
  44.9 10.7 %shard_map.241 = (f32[1024,1024]{1,0:T(8,128)}, bf16[1024,1024]{1,0:T(8,128)(2,1)}) custom-call(bf16[1024,1024]{1,0:T(8,128)(2,1)} %bitcast.66, bf16[1024,1024]{1,0:T(8,128)(2,1)} %get-tuple-element.43.m_ref.o_ref.a_ref, bf16[1024,1024]{1,0:T(8,128)(2,1)} %w_ref.3, f32[1,1024]{1,0:T(1,128)} %bitcast.93, f32[1,1024]{1,0:T(1,128)} %bitcast.98, ...), custom_call_target="tpu_custom_call" | custom-call | tf_op jit(solution)/shard_map/pallas_call | solution.py:330
  55.6 32.0 %all_to_all.20 = bf16[8,128,1024]{2,1,0:T(8,128)(2,1)} all-to-all(bf16[8,128,1024]{2,1,0:T(8,128)(2,1)} %bitcast.85), channel_id=1, replica_groups=mesh['rep'=4,'exp'=8] {'exp'}, dimensions={0} | all-to-all | bytes 4194304 | tf_op jit(solution)/shard_map/all_to_all | solution.py:615
  87.6 29.9 %all_to_all.21 = bf16[8,128,1024]{2,1,0:T(8,128)(2,1)} all-to-all(bf16[8,128,1024]{2,1,0:T(8,128)(2,1)S(1)} %bitcast.84), channel_id=1, replica_groups=mesh['rep'=4,'exp'=8] {'exp'}, dimensions={0} | all-to-all | bytes 4194304 | tf_op jit(solution)/shard_map/all_to_all | solution.py:615
  117.6 33.6 %shard_map.242 = (bf16[1024,1024]{1,0:T(8,128)(2,1)}, bf16[1024,4096]{1,0:T(8,128)(2,1)}) custom-call(bf16[1024,1024]{1,0:T(8,128)(2,1)} %bitcast.68, bf16[1024,1024]{1,0:T(8,128)(2,1)} %bitcast.72, bf16[4096,1024]{1,0:T(8,128)(2,1)} %bitcast.76, bf16[4096,1024]{1,0:T(8,128)(2,1)} %bitcast.63), custom_call_target="tpu_custom_call" | custom-call | tf_op jit(solution)/shard_map/pallas_call | solution.py:381
  151.2 31.0 %all_to_all.22 = bf16[8,128,1024]{2,1,0:T(8,128)(2,1)} all-to-all(bf16[8,128,1024]{2,1,0:T(8,128)(2,1)} %bitcast.86), channel_id=1, replica_groups=mesh['rep'=4,'exp'=8] {'exp'}, dimensions={0} | all-to-all | bytes 4194304 | tf_op jit(solution)/shard_map/all_to_all | solution.py:615
  182.2 12.5 %shard_map.245 = (f32[1024,1024]{1,0:T(8,128)}, bf16[1024,1024]{1,0:T(8,128)(2,1)}, bf16[1024,1024]{1,0:T(8,128)(2,1)}, f32[1,1024]{1,0:T(1,128)}, f32[1,1024]{1,0:T(1,128)}) custom-call(bf16[1024,1024]{1,0:T(8,128)(2,1)} %bitcast.80, f32[8,1024]{1,0:T(8,128)} %get-tuple-element.44.place_ref, f32[1024,1024]{1,0:T(8,128)} %get-tuple-element.48.mid_ref, ...), custom_call_target="tpu_custom_call" | custom-call | tf_op jit(solution)/shard_map/pallas_call | solution.py:487
  194.7 6.1 shard_map.249
  204.4 31.1 %shard_map.246 = (bf16[1024,1024]{1,0:T(8,128)(2,1)}, bf16[1024,1024]{1,0:T(8,128)(2,1)}, bf16[1024,1024]{1,0:T(8,128)(2,1)}) custom-call(s32[1]{0:T(128)S(6)} %copy.35.len_ref, bf16[1024,1024]{1,0:T(8,128)(2,1)} %get-tuple-element.40.q_ref, bf16[1024,1024]{1,0:T(8,128)(2,1)} %get-tuple-element.41.k_ref, bf16[1024,1024]{1,0:T(8,128)(2,1)} %get-tuple-element.42.v_ref, ...), custom_call_target="tpu_custom_call" | custom-call | tf_op jit(solution)/shard_map/pallas_call | solution.py:301
  235.4 11.3 %shard_map.248 = (bf16[1024,1024]{1,0:T(8,128)(2,1)}, bf16[1024,1024]{1,0:T(8,128)(2,1)}, bf16[1024,1024]{1,0:T(8,128)(2,1)}) custom-call(bf16[1024,1024]{1,0:T(8,128)(2,1)} %get-tuple-element.61.a_ref, bf16[1024,1024]{1,0:T(8,128)(2,1)} %get-tuple-element.52.gq_ref.refs_0_, bf16[1024,1024]{1,0:T(8,128)(2,1)} %get-tuple-element.53.gk_ref.refs_1_, ...), custom_call_target="tpu_custom_call" | custom-call | tf_op jit(solution)/shard_map/pallas_call | solution.py:517
  246.7 6.0 copy_bitcast_fusion
  256.9 6.6 collective-permute-start
  263.5 4.0 collective-permute-start.6
  267.4 37.5 %collective-permute-done.1 = bf16[1024,1024]{1,0:T(8,128)(2,1)} collective-permute-done((bf16[1024,1024]{1,0:T(8,128)(2,1)S(1)}, bf16[1024,1024]{1,0:T(8,128)(2,1)}, u32[]{:S(2)}, u32[]{:S(2)}) %collective-permute-start.1) | collective-permute-done | bytes 2097184 | tf_op jit(solution)/shard_map/ppermute | solution.py:623
  306.2 43.7 %collective-permute-done.7 = bf16[1024,1024]{1,0:T(8,128)(2,1)} collective-permute-done((bf16[1024,1024]{1,0:T(8,128)(2,1)}, bf16[1024,1024]{1,0:T(8,128)(2,1)}, u32[]{:S(2)}, u32[]{:S(2)}) %collective-permute-start.7) | collective-permute-done | bytes 2097184 | tf_op jit(solution)/shard_map/ppermute | solution.py:623
  351.1 5.9 collective-permute-start.4
  357.0 14.2 %shard_map.243 = bf16[1024,1024]{1,0:T(8,128)(2,1)} custom-call(bf16[1024,4096]{1,0:T(8,128)(2,1)} %get-tuple-element.47.a_ref, bf16[4096,1024]{1,0:T(8,128)(2,1)} %bitcast.64), custom_call_target="tpu_custom_call" | custom-call | tf_op jit(solution)/shard_map/pallas_call | solution.py:399
  371.2 3.6 all-to-all-start.2
  374.9 3.9 collective-permute-start.10
  378.8 15.9 %collective-permute-done.2 = bf16[1024,1024]{1,0:T(8,128)(2,1)} collective-permute-done((bf16[1024,1024]{1,0:T(8,128)(2,1)}, bf16[1024,1024]{1,0:T(8,128)(2,1)}, u32[]{:S(2)}, u32[]{:S(2)}) %collective-permute-start.2) | collective-permute-done | bytes 2097184 | tf_op jit(solution)/shard_map/ppermute | solution.py:623
  396.1 43.6 %collective-permute-done.8 = bf16[1024,1024]{1,0:T(8,128)(2,1)} collective-permute-done((bf16[1024,1024]{1,0:T(8,128)(2,1)}, bf16[1024,1024]{1,0:T(8,128)(2,1)}, u32[]{:S(2)}, u32[]{:S(2)}) %collective-permute-start.8) | collective-permute-done | bytes 2097184 | tf_op jit(solution)/shard_map/ppermute | solution.py:623
  448.8 7.0 shard_map.244
  455.8 14.5 %shard_map.247 = (f32[1024,1024]{1,0:T(8,128)}, f32[1,1024]{1,0:T(1,128)}, f32[1,1024]{1,0:T(1,128)}) custom-call(bf16[1024,1024]{1,0:T(8,128)(2,1)} %get-tuple-element.52.gq_ref.refs_0_, bf16[1024,1024]{1,0:T(8,128)(2,1)} %get-tuple-element.53.gk_ref.refs_1_, bf16[1024,1024]{1,0:T(8,128)(2,1)} %get-tuple-element.54.gv_ref.refs_2_, ...), custom_call_target="tpu_custom_call" | custom-call | tf_op jit(solution)/shard_map/pallas_call | solution.py:550
  471.0 77.4 %psum.7 = f32[4,1024]{1,0:T(4,128)S(1)} all-reduce(f32[4,1024]{1,0:T(4,128)S(1)} %pad_maximum_fusion.1), channel_id=1, replica_groups=mesh['rep'=4,'exp'=8] {'rep','exp'}, use_global_device_ids=true, to_apply=%region_0.1 | all-reduce | flops 4096 | bytes 32768 | tf_op jit(solution)/shard_map/psum | solution.py:674
  548.4 3.7 collective-permute-start.5
  552.7 4.5 collective-permute-start.11
  563.7 13.7 %reduce-scatter.11.cloned.1.call-done = bf16[1,32,1024]{2,1,0:T(8,128)(2,1)} async-done(((bf16[4,32,1024]{2,1,0:T(8,128)(2,1)}), bf16[1,32,1024]{2,1,0:T(8,128)(2,1)}) %reduce-scatter.11.cloned.1.call-update) | async-done | bytes 65552 | tf_op jit(solution)/shard_map/reduce_scatter | solution.py:666
  585.2 29.9 %collective-permute-done.5 = bf16[1024,1024]{1,0:T(8,128)(2,1)S(1)} collective-permute-done((bf16[1024,1024]{1,0:T(8,128)(2,1)}, bf16[1024,1024]{1,0:T(8,128)(2,1)S(1)}, u32[]{:S(2)}, u32[]{:S(2)}) %collective-permute-start.5) | collective-permute-done | bytes 2097184 | tf_op jit(solution)/shard_map/ppermute | solution.py:622
  618.3 39.8 %collective-permute-done.11 = bf16[1024,1024]{1,0:T(8,128)(2,1)} collective-permute-done((bf16[1024,1024]{1,0:T(8,128)(2,1)}, bf16[1024,1024]{1,0:T(8,128)(2,1)}, u32[]{:S(2)}, u32[]{:S(2)}) %collective-permute-start.11) | collective-permute-done | bytes 2097184 | tf_op jit(solution)/shard_map/ppermute | solution.py:622
  661.3 43.0 %shard_map.250 = (f32[1024,1024]{1,0:T(8,128)}, f32[1024,1024]{1,0:T(8,128)}) custom-call(bf16[1024,1024]{1,0:T(8,128)(2,1)} %bitcast.69, bf16[1024,1024]{1,0:T(8,128)(2,1)} %broadcast_select_fusion.5.refs_1_, bf16[1024,1024]{1,0:T(8,128)(2,1)} %broadcast_select_fusion.3.refs_2_, bf16[1024,1024]{1,0:T(8,128)(2,1)} %broadcast_select_fusion.1.refs_3_, ...), custom_call_target="tpu_custom_call" | custom-call | tf_op jit(solution)/shard_map/pallas_call | solution.py:448
  (49 shorter events, 45.7 us)
Async XLA Ops:
  7.2 550.0 %reduce-scatter.9.cloned.1.call-start = ((), (), s32[]{:S(2)}) async-start(), calls=%async_computation.10 | async-start | bytes 2359296 | tf_op jit(solution)/shard_map/reduce_scatter | solution.py:663
  55.6 32.0 %copy-start.2 = (bf16[1024,1024]{1,0:T(8,128)(2,1)S(1)}, bf16[1024,1024]{1,0:T(8,128)(2,1)}, u32[]{:S(2)}) copy-start(bf16[1024,1024]{1,0:T(8,128)(2,1)} %get-tuple-element.46) | copy-start | bytes 6291460
  204.1 359.5 %reduce-scatter.5.cloned.1.call-start = ((), (), s32[]{:S(2)}) async-start(), calls=%async_computation.8 | async-start | bytes 7077888 | tf_op jit(solution)/shard_map/reduce_scatter | solution.py:663
  252.7 1.6 copy-start
  254.3 50.6 %collective-permute-start.1 = (bf16[1024,1024]{1,0:T(8,128)(2,1)S(1)}, bf16[1024,1024]{1,0:T(8,128)(2,1)}, u32[]{:S(2)}, u32[]{:S(2)}) collective-permute-start(bf16[1024,1024]{1,0:T(8,128)(2,1)S(1)} %bitcast.70), channel_id=1, source_target_pairs={{8,0},{16,8},{24,16},{9,1},{17,9},{25,17},{10,2},{18,10},{26,18},{... | collective-permute-start | bytes 6291464 | tf_op jit(solution)/shard_map/ppermute | solution.py:623
  255.6 94.3 %collective-permute-start.7 = (bf16[1024,1024]{1,0:T(8,128)(2,1)}, bf16[1024,1024]{1,0:T(8,128)(2,1)}, u32[]{:S(2)}, u32[]{:S(2)}) collective-permute-start(bf16[1024,1024]{1,0:T(8,128)(2,1)} %bitcast.73), channel_id=1, source_target_pairs={{8,0},{16,8},{24,16},{9,1},{17,9},{25,17},{10,2},{18,10},{26,18},{... | collective-permute-start | bytes 6291464 | tf_op jit(solution)/shard_map/ppermute | solution.py:623
  256.9 94.3 %collective-permute-start = (bf16[1024,1024]{1,0:T(8,128)(2,1)S(1)}, bf16[1024,1024]{1,0:T(8,128)(2,1)}, u32[]{:S(2)}, u32[]{:S(2)}) collective-permute-start(bf16[1024,1024]{1,0:T(8,128)(2,1)S(1)} %bitcast.71), channel_id=1, source_target_pairs={{0,8},{8,16},{16,24},{1,9},{9,17},{17,25},{2,10},{10,18},{18,26},{... | collective-permute-start | bytes 6291464 | tf_op jit(solution)/shard_map/ppermute | solution.py:622
  263.5 111.4 %collective-permute-start.6 = (bf16[1024,1024]{1,0:T(8,128)(2,1)}, bf16[1024,1024]{1,0:T(8,128)(2,1)}, u32[]{:S(2)}, u32[]{:S(2)}) collective-permute-start(bf16[1024,1024]{1,0:T(8,128)(2,1)} %bitcast.74), channel_id=1, source_target_pairs={{0,8},{8,16},{16,24},{1,9},{9,17},{17,25},{2,10},{10,18},{18,26},{... | collective-permute-start | bytes 6291464 | tf_op jit(solution)/shard_map/ppermute | solution.py:622
  304.9 89.9 %collective-permute-start.2 = (bf16[1024,1024]{1,0:T(8,128)(2,1)}, bf16[1024,1024]{1,0:T(8,128)(2,1)}, u32[]{:S(2)}, u32[]{:S(2)}) collective-permute-start(bf16[1024,1024]{1,0:T(8,128)(2,1)} %collective-permute-done.1), channel_id=1, source_target_pairs={{8,0},{16,8},{24,16},{9,1},{17,9},{25,17},{10,2},{18,10},{26,18},{... | collective-permute-start | bytes 6291464 | tf_op jit(solution)/shard_map/ppermute | solution.py:623
  349.8 89.9 %collective-permute-start.8 = (bf16[1024,1024]{1,0:T(8,128)(2,1)}, bf16[1024,1024]{1,0:T(8,128)(2,1)}, u32[]{:S(2)}, u32[]{:S(2)}) collective-permute-start(bf16[1024,1024]{1,0:T(8,128)(2,1)} %collective-permute-done.7), channel_id=1, source_target_pairs={{8,0},{16,8},{24,16},{9,1},{17,9},{25,17},{10,2},{18,10},{26,18},{... | collective-permute-start | bytes 6291464 | tf_op jit(solution)/shard_map/ppermute | solution.py:623
  351.1 197.3 %collective-permute-start.4 = (bf16[1024,1024]{1,0:T(8,128)(2,1)}, bf16[1024,1024]{1,0:T(8,128)(2,1)}, u32[]{:S(2)}, u32[]{:S(2)}) collective-permute-start(bf16[1024,1024]{1,0:T(8,128)(2,1)} %collective-permute-done), channel_id=1, source_target_pairs={{0,8},{8,16},{16,24},{1,9},{9,17},{17,25},{2,10},{10,18},{18,26},{... | collective-permute-start | bytes 6291464 | tf_op jit(solution)/shard_map/ppermute | solution.py:622
  371.2 76.2 %all-to-all-start.2 = ((bf16[8,128,1024]{2,1,0:T(8,128)(2,1)}), bf16[8,128,1024]{2,1,0:T(8,128)(2,1)S(1)}, u32[]{:S(2)}, u32[]{:S(2)}) async-start(bf16[8,128,1024]{2,1,0:T(8,128)(2,1)} %bitcast.79), calls=%async_computation.2 | async-start | bytes 4194304 | tf_op jit(solution)/shard_map/all_to_all | solution.py:615
  374.8 202.6 %reduce-scatter.11.cloned.1.call-start = ((), (), s32[]{:S(2)}) async-start(), calls=%async_computation.11 | async-start | bytes 327680 | tf_op jit(solution)/shard_map/reduce_scatter | solution.py:666
  374.9 177.8 %collective-permute-start.10 = (bf16[1024,1024]{1,0:T(8,128)(2,1)}, bf16[1024,1024]{1,0:T(8,128)(2,1)}, u32[]{:S(2)}, u32[]{:S(2)}) collective-permute-start(bf16[1024,1024]{1,0:T(8,128)(2,1)} %collective-permute-done.6), channel_id=1, source_target_pairs={{0,8},{8,16},{16,24},{1,9},{9,17},{17,25},{2,10},{10,18},{18,26},{... | collective-permute-start | bytes 6291464 | tf_op jit(solution)/shard_map/ppermute | solution.py:622
  394.8 184.1 %collective-permute-start.3 = (bf16[1024,1024]{1,0:T(8,128)(2,1)}, bf16[1024,1024]{1,0:T(8,128)(2,1)}, u32[]{:S(2)}, u32[]{:S(2)}) collective-permute-start(bf16[1024,1024]{1,0:T(8,128)(2,1)} %collective-permute-done.2), channel_id=1, source_target_pairs={{8,0},{16,8},{24,16},{9,1},{17,9},{25,17},{10,2},{18,10},{26,18},{... | collective-permute-start | bytes 6291464 | tf_op jit(solution)/shard_map/ppermute | solution.py:623
  439.7 142.3 %collective-permute-start.9 = (bf16[1024,1024]{1,0:T(8,128)(2,1)}, bf16[1024,1024]{1,0:T(8,128)(2,1)}, u32[]{:S(2)}, u32[]{:S(2)}) collective-permute-start(bf16[1024,1024]{1,0:T(8,128)(2,1)} %collective-permute-done.8), channel_id=1, source_target_pairs={{8,0},{16,8},{24,16},{9,1},{17,9},{25,17},{10,2},{18,10},{26,18},{... | collective-permute-start | bytes 6291464 | tf_op jit(solution)/shard_map/ppermute | solution.py:623
  447.4 1.3 copy-start.1
  455.8 14.5 %copy-start.3 = (f32[1,1024]{1,0:T(1,128)S(1)}, f32[1,1024]{1,0:T(1,128)}, u32[]{:S(2)}) copy-start(f32[1,1024]{1,0:T(1,128)} %get-tuple-element.59) | copy-start | bytes 12292
  455.8 14.5 %copy-start.4 = (f32[1,1024]{1,0:T(1,128)S(1)}, f32[1,1024]{1,0:T(1,128)}, u32[]{:S(2)}) copy-start(f32[1,1024]{1,0:T(1,128)} %get-tuple-element.60) | copy-start | bytes 12292
  548.4 66.8 %collective-permute-start.5 = (bf16[1024,1024]{1,0:T(8,128)(2,1)}, bf16[1024,1024]{1,0:T(8,128)(2,1)S(1)}, u32[]{:S(2)}, u32[]{:S(2)}) collective-permute-start(bf16[1024,1024]{1,0:T(8,128)(2,1)} %collective-permute-done.4), channel_id=1, source_target_pairs={{0,8},{8,16},{16,24},{1,9},{9,17},{17,25},{2,10},{10,18},{18,26},{... | collective-permute-start | bytes 6291464 | tf_op jit(solution)/shard_map/ppermute | solution.py:622
  552.7 105.4 %collective-permute-start.11 = (bf16[1024,1024]{1,0:T(8,128)(2,1)}, bf16[1024,1024]{1,0:T(8,128)(2,1)}, u32[]{:S(2)}, u32[]{:S(2)}) collective-permute-start(bf16[1024,1024]{1,0:T(8,128)(2,1)} %collective-permute-done.10), channel_id=1, source_target_pairs={{0,8},{8,16},{16,24},{1,9},{9,17},{17,25},{2,10},{10,18},{18,26},{... | collective-permute-start | bytes 6291464 | tf_op jit(solution)/shard_map/ppermute | solution.py:622
  557.2 147.2 %reduce-scatter.7.cloned.1.call-start = ((), (), s32[]{:S(2)}) async-start(), calls=%async_computation.9 | async-start | bytes 983040 | tf_op jit(solution)/shard_map/reduce_scatter | solution.py:666
Sparse Core Ops, SparseCore 0:
  204.2 41.0 reduce-scatter.8
  252.8 61.6 reduce-scatter.4
  557.3 20.0 reduce-scatter.10
  579.6 30.4 reduce-scatter.6

commit v2 on v1

--- a/solution.py
+++ b/solution.py
@@ -13,11 +13,92 @@
 MASKED = -1e30
 epsilon = 1e-05
 bf16, f32 = jnp.bfloat16, jnp.float32
+MESH = pl.DeviceIdType.MESH
+ANY = pl.BlockSpec(memory_space=pl.ANY)
 VMEM_BYTES = 56 * 1024 * 1024
-
-
-def params():
-    return pltpu.CompilerParams(vmem_limit_bytes=VMEM_BYTES)
+PARTS = 4
+
+
+def params(collective_id=None):
+    if collective_id is None:
+        return pltpu.CompilerParams(vmem_limit_bytes=VMEM_BYTES)
+    return pltpu.CompilerParams(
+        vmem_limit_bytes=VMEM_BYTES, collective_id=collective_id, has_side_effects=True
+    )
+
+
+def launch(kernel, operands, in_specs, micros, after=(), collective_id=None, **options):
+    count = len(operands)
+
+    def run(*refs):
+        kernel(*refs[:count], *refs[count + len(after) :])
+
+    return pl.pallas_call(
+        run,
+        in_specs=list(in_specs) + [pl.BlockSpec(memory_space=pl.ANY)] * len(after),
+        compiler_params=params(collective_id),
+        cost_estimate=pl.CostEstimate(
+            flops=int(micros * 1.1e9), bytes_accessed=int(micros * 3.5e6), transcendentals=0
+        ),
+        **options,
+    )(*operands, *after)
+
+
+def greet(groups):
+    me = lax.axis_index("exp")
+    barrier = pltpu.get_barrier_semaphore()
+
+    def tell(step, carry):
+        peer = lax.rem(me + step, groups)
+        pl.semaphore_signal(barrier, inc=1, device_id={"exp": peer}, device_id_type=MESH)
+        return carry
+
+    lax.fori_loop(1, groups, tell, 0)
+    pl.semaphore_wait(barrier, groups - 1)
+
+
+def remote(source, target, send_sem, recv_sem, peer):
+    return pltpu.make_async_remote_copy(
+        src_ref=source,
+        dst_ref=target,
+        send_sem=send_sem,
+        recv_sem=recv_sem,
+        device_id={"exp": peer},
+        device_id_type=MESH,
+    )
+
+
+def start_exchange(send_ref, recv_ref, send_sems, recv_sems):
+    groups = send_ref.shape[0]
+    me = lax.axis_index("exp")
+    greet(groups)
+    pltpu.make_async_copy(send_ref.at[me], recv_ref.at[me], recv_sems.at[me]).start()
+
+    def send(step, carry):
+        peer = lax.rem(me + step, groups)
+        remote(send_ref.at[peer], recv_ref.at[me], send_sems.at[peer], recv_sems.at[me], peer).start()
+        return carry
+
+    lax.fori_loop(1, groups, send, 0)
+
+
+def finish_exchange(send_ref, recv_ref, send_sems, recv_sems):
+    groups = send_ref.shape[0]
+    me = lax.axis_index("exp")
+    pltpu.make_async_copy(send_ref.at[me], recv_ref.at[me], recv_sems.at[me]).wait()
+
+    def wait(step, carry):
+        peer = lax.rem(me + step, groups)
+        copy = remote(send_ref.at[peer], recv_ref.at[peer], send_sems.at[peer], recv_sems.at[peer], peer)
+        copy.wait_send()
+        copy.wait_recv()
+        return carry
+
+    lax.fori_loop(1, groups, wait, 0)
+
+
+def exchange_scratch(send):
+    return [pltpu.SemaphoreType.DMA((send.shape[0],))] * 2
 
 
 def shape(dims, kind):
@@ -68,7 +149,9 @@
     return hidden * share, slope
 
 
-def route_kernel(len_ref, ids_ref, table_ref, cot_ref, place_ref, send_ref, *, groups, capacity):
+def route_kernel(
+    len_ref, ids_ref, table_ref, cot_ref, place_ref, send_a_ref, send_b_ref, *, groups, capacity
+):
     seq_len = ids_ref.shape[1]
     slot_total = groups * capacity
     high_count, low_count = table_ref.shape
@@ -91,7 +174,11 @@
     slot = jnp.sum(before * chosen, axis=0, keepdims=True)
     place = jnp.where(valid & (slot < capacity), expert * capacity + slot, float(slot_total))
     place_ref[...] = jnp.broadcast_to(place, place_ref.shape)
-    send_ref[...] = nn(slot_pick(place, slot_total), cot_ref[...]).astype(bf16)
+    sent = nn(slot_pick(place, slot_total), cot_ref[...]).astype(bf16)
+    sent = sent.reshape(groups, capacity, sent.shape[1])
+    half = capacity // 2
+    send_a_ref[...] = sent[:, :half]
+    send_b_ref[...] = sent[:, half:]
 
 
 def slot_pick(place_row, slot_total):
@@ -105,26 +192,33 @@
     return jnp.where(slots == column, 1.0, 0.0).astype(bf16)
 
 
-def route(lengths, ids, table, cotangent, groups, capacity):
+def route(lengths, ids, table, cotangent, groups, capacity, after=()):
     rows, width = cotangent.shape
-    return pl.pallas_call(
+    return launch(
         functools.partial(route_kernel, groups=groups, capacity=capacity),
-        in_specs=[
+        (lengths, ids, table, cotangent,),
+        [
             pl.BlockSpec(memory_space=pltpu.SMEM),
             whole(ids),
             whole(table),
             whole(cotangent),
         ],
-        out_specs=[
-            pl.BlockSpec((8, rows), lambda: (0, 0)),
-            pl.BlockSpec((groups * capacity, width), lambda: (0, 0)),
-        ],
-        out_shape=[shape((8, rows), f32), shape((groups * capacity, width), bf16)],
-        compiler_params=params(),
-    )(lengths, ids, table, cotangent)
-
-
-def project_kernel(x_ref, gain_ref, shift_ref, wq_ref, wk_ref, wv_ref, n_ref, q_ref, k_ref, v_ref):
+        10,
+        after,
+        out_specs=[pl.BlockSpec((8, rows), lambda: (0, 0))]
+        + [pl.BlockSpec((groups, capacity // 2, width), lambda: (0, 0, 0))] * 2,
+        out_shape=[shape((8, rows), f32)] + [shape((groups, capacity // 2, width), bf16)] * 2,
+    )
+
+
+def project_kernel(
+    x_ref, gain_ref, shift_ref, wq_ref, wk_ref, wv_ref, send_ref,
+    n_ref, q_ref, k_ref, v_ref, recv_ref, send_sems, recv_sems,
+):
+    @pl.when(pl.program_id(0) == 0)
+    def _():
+        start_exchange(send_ref, recv_ref, send_sems, recv_sems)
+
     normal, _ = normalize(x_ref[...].astype(f32))
     normed = (normal * gain_ref[...] + shift_ref[...]).astype(bf16)
     n_ref[...] = normed
@@ -132,17 +226,25 @@
     k_ref[...] = nn(normed, wk_ref[...]).astype(bf16)
     v_ref[...] = nn(normed, wv_ref[...]).astype(bf16)
 
-
-def project(x, gain, shift, wq, wk, wv, block=256):
+    @pl.when(pl.program_id(0) == pl.num_programs(0) - 1)
+    def _():
+        finish_exchange(send_ref, recv_ref, send_sems, recv_sems)
+
+
+def project(x, gain, shift, wq, wk, wv, send, block=256, after=()):
     rows, width = x.shape
-    return pl.pallas_call(
+    return launch(
         project_kernel,
+        (x, gain, shift, wq, wk, wv, send),
+        [row_spec(block, width)] + [whole(a) for a in (gain, shift, wq, wk, wv)] + [ANY],
+        16,
+        after,
+        collective_id=2,
         grid=(rows // block,),
-        in_specs=[row_spec(block, width)] + [whole(a) for a in (gain, shift, wq, wk, wv)],
-        out_specs=[row_spec(block, width)] * 4,
-        out_shape=[shape((rows, width), bf16)] * 4,
-        compiler_params=params(),
-    )(x, gain, shift, wq, wk, wv)
+        out_specs=[row_spec(block, width)] * 4 + [ANY],
+        out_shape=[shape((rows, width), bf16)] * 4 + [shape(send.shape, bf16)],
+        scratch_shapes=exchange_scratch(send),
+    )
 
 
 def head_parts(length, block, seq_len):
@@ -154,7 +256,14 @@
     return lane // HEAD_DIM, lane % HEAD_DIM == 0, bias, down <= across
 
 
-def attend_kernel(len_ref, q_ref, k_ref, v_ref, o_ref, log_ref, *, block, pairs):
+def attend_kernel(
+    len_ref, q_ref, k_ref, v_ref, send_ref, o_ref, log_ref, recv_ref, send_sems, recv_sems,
+    *, block, pairs,
+):
+    @pl.when(pl.program_id(0) == 0)
+    def _():
+        start_exchange(send_ref, recv_ref, send_sems, recv_sems)
+
     seq_len = q_ref.shape[0]
     factor = HEAD_DIM**-0.5 * math.log2(math.e)
     half, first_lane, bias, causal = head_parts(len_ref[0], block, seq_len)
@@ -205,23 +314,40 @@
         behind = soften(scores, j)
     finish(*behind, *order[-1])
 
-
-def attend(lengths, q, k, v, block=256, pairs=2):
+    @pl.when(pl.program_id(0) == pl.num_programs(0) - 1)
+    def _():
+        finish_exchange(send_ref, recv_ref, send_sems, recv_sems)
+
+
+def attend(lengths, q, k, v, send, block=256, pairs=2, after=()):
     rows, width = q.shape
     lanes = pl.BlockSpec((rows, pairs * PAIR), lambda i: (0, i))
-    return pl.pallas_call(
+    return launch(
         functools.partial(attend_kernel, block=block, pairs=pairs),
+        (lengths, q, k, v, send),
+        [pl.BlockSpec(memory_space=pltpu.SMEM)] + [lanes] * 3 + [ANY],
+        24,
+        after,
+        collective_id=0,
         grid=(width // (pairs * PAIR),),
-        in_specs=[pl.BlockSpec(memory_space=pltpu.SMEM)] + [lanes] * 3,
-        out_specs=[lanes, pl.BlockSpec((pairs, 2, rows), lambda i: (i, 0, 0))],
-        out_shape=[shape((rows, width), bf16), shape((width // PAIR, 2, rows), f32)],
-        compiler_params=params(),
-    )(lengths, q, k, v)
+        out_specs=[lanes, pl.BlockSpec((pairs, 2, rows), lambda i: (i, 0, 0)), ANY],
+        out_shape=[
+            shape((rows, width), bf16),
+            shape((width // PAIR, 2, rows), f32),
+            shape(send.shape, bf16),
+        ],
+        scratch_shapes=exchange_scratch(send),
+    )
 
 
 def attend_back_kernel(
-    len_ref, q_ref, k_ref, v_ref, o_ref, g_ref, log_ref, dq_ref, dk_ref, dv_ref, *, block, pairs
+    len_ref, q_ref, k_ref, v_ref, o_ref, g_ref, log_ref, send_ref,
+    dq_ref, dk_ref, dv_ref, recv_ref, send_sems, recv_sems, *, block, pairs,
 ):
+    @pl.when(pl.program_id(0) == 0)
+    def _():
+        start_exchange(send_ref, recv_ref, send_sems, recv_sems)
+
     seq_len = q_ref.shape[0]
     blocks = seq_len // block
     scale = HEAD_DIM**-0.5
@@ -294,20 +420,28 @@
         behind = shares_of(*now, h, i)
     finish(*behind, *order[-1])
 
-
-def attend_back(lengths, q, k, v, mixed, grad_mixed, logs, block=256, pairs=2):
+    @pl.when(pl.program_id(0) == pl.num_programs(0) - 1)
+    def _():
+        finish_exchange(send_ref, recv_ref, send_sems, recv_sems)
+
+
+def attend_back(lengths, q, k, v, mixed, grad_mixed, logs, send, block=256, pairs=2, after=()):
     rows, width = q.shape
     lanes = pl.BlockSpec((rows, pairs * PAIR), lambda i: (0, i))
-    return pl.pallas_call(
+    return launch(
         functools.partial(attend_back_kernel, block=block, pairs=pairs),
+        (lengths, q, k, v, mixed, grad_mixed, logs, send),
+        [pl.BlockSpec(memory_space=pltpu.SMEM)]
+        + [lanes] * 5
+        + [pl.BlockSpec((pairs, 2, rows), lambda i: (i, 0, 0)), ANY],
+        31,
+        after,
+        collective_id=3,
         grid=(width // (pairs * PAIR),),
-        in_specs=[pl.BlockSpec(memory_space=pltpu.SMEM)]
-        + [lanes] * 5
-        + [pl.BlockSpec((pairs, 2, rows), lambda i: (i, 0, 0))],
-        out_specs=[lanes] * 3,
-        out_shape=[shape((rows, width), bf16)] * 3,
-        compiler_params=params(),
-    )(lengths, q, k, v, mixed, grad_mixed, logs)
+        out_specs=[lanes] * 3 + [ANY],
+        out_shape=[shape((rows, width), bf16)] * 3 + [shape(send.shape, bf16)],
+        scratch_shapes=exchange_scratch(send),
+    )
 
 
 def middle_kernel(x_ref, m_ref, w_ref, gain_ref, shift_ref, place_ref, mid_ref, send_ref, sent):
@@ -324,110 +458,208 @@
         send_ref[...] = nn(pick, sent[...]).astype(bf16)
 
 
-def middle_and_send(x, mixed, w_output, gain, shift, place, slot_total, block=256):
+def middle_and_send(x, mixed, w_output, gain, shift, place, slot_total, block=256, after=()):
     rows, width = x.shape
     blocked = row_spec(block, width)
-    return pl.pallas_call(
+    return launch(
         middle_kernel,
+        (x, mixed, w_output, gain, shift, place,),
+        [blocked, blocked] + [whole(a) for a in (w_output, gain, shift, place)],
+        10,
+        after,
         grid=(rows // block,),
-        in_specs=[blocked, blocked] + [whole(a) for a in (w_output, gain, shift, place)],
         out_specs=[blocked, pl.BlockSpec((slot_total, width), lambda i: (0, 0))],
         out_shape=[shape((rows, width), f32), shape((slot_total, width), bf16)],
         scratch_shapes=[pltpu.VMEM((rows, width), bf16)],
-        compiler_params=params(),
-    )(x, mixed, w_output, gain, shift, place)
-
-
-def expert_kernel(x_ref, g_ref, in_ref, out_ref, slots_ref, act_ref, total, *, chunk):
-    step = pl.program_id(0)
-    count = x_ref.shape[0] // chunk
-
-    @pl.when(step == 0)
-    def _():
-        total[...] = jnp.zeros_like(total)
-
-    def rows(r):
-        return slice(r * chunk, (r + 1) * chunk)
-
-    def first(r):
-        return nt(x_ref[rows(r)], in_ref[...]), nt(g_ref[rows(r)], out_ref[...])
-
-    def second(hidden, grad_activated, r):
-        activated, slope = gelu_parts(hidden)
-        act_ref[rows(r)] = activated.astype(bf16)
-        return (grad_activated * slope).astype(bf16)
-
-    def third(grad_hidden, r):
-        total[rows(r)] += nn(grad_hidden, in_ref[...])
-
-    ahead, behind = first(0), None
-    for r in range(count):
-        now = ahead
-        if r + 1 < count:
-            ahead = first(r + 1)
-        if behind is not None:
-            third(behind, r - 1)
-        behind = second(*now, r)
-    third(behind, count - 1)
-
-    @pl.when(step == pl.num_programs(0) - 1)
-    def _():
-        slots_ref[...] = total[...].astype(bf16)
-
-
-def expert_main(x, g, w_in, w_out, block=1024, chunk=256):
-    rows, width = x.shape
+    )
+
+
+def expert_kernel(
+    send_ref, ga_ref, gb_ref, in_hbm, out_hbm, back_ref, result_ref, arrived_0, arrived_1, arrived_2, arrived_3,
+    w_in, w_out, x_all, slots_all, result_all,
+    w_sems, send_sems, recv_sems, back_sems, back_recv, keep_sems,
+    *, rows, sub,
+):
+    groups, capacity, width = send_ref.shape
+    me = lax.axis_index("exp")
     units = w_in.shape[0]
-    return pl.pallas_call(
-        functools.partial(expert_kernel, chunk=chunk),
-        grid=(units // block,),
-        in_specs=[whole(x), whole(g), row_spec(block, width), row_spec(block, width)],
-        out_specs=[whole(x), pl.BlockSpec((rows, block), lambda i: (0, i))],
-        out_shape=[shape((rows, width), bf16), shape((rows, units), bf16)],
-        scratch_shapes=[pltpu.VMEM((rows, width), f32)],
-        compiler_params=params(),
-    )(x, g, w_in, w_out)
-
-
-def result_kernel(a_ref, w_ref, o_ref):
-    o_ref[...] = nn(a_ref[...], w_ref[...]).astype(bf16)
-
-
-def expert_result(activated, w_out, block=256):
-    rows, units = activated.shape
-    width = w_out.shape[1]
-    return pl.pallas_call(
-        result_kernel,
-        grid=(rows // block,),
-        in_specs=[row_spec(block, units), whole(w_out)],
-        out_specs=row_spec(block, width),
-        out_shape=shape((rows, width), bf16),
-        compiler_params=params(),
-    )(activated, w_out)
-
-
-def expert_grad_kernel(*refs, count, sub):
-    x_refs, g_refs = refs[:count], refs[count : 2 * count]
-    in_ref, out_ref, gin_ref, gout_ref = refs[2 * count :]
-    order = [(r, p) for r in range(in_ref.shape[0] // sub) for p in range(count)]
-    sums = [None]
+    sources = rows // capacity
+    blocks = groups // sources
+    mine = me // sources
+    count = units // sub
+    loads = []
+    for f in range(count):
+        part = slice(f * sub, (f + 1) * sub)
+        pair = [
+            pltpu.make_async_copy(hbm.at[part], vmem.at[part], w_sems.at[n, f])
+            for n, (hbm, vmem) in enumerate(((in_hbm, w_in), (out_hbm, w_out)))
+        ]
+        for load in pair:
+            load.start()
+        loads.append(pair)
+    greet(groups)
+
+    def send_block(j, carry):
+        block = lax.rem(mine + blocks - j, blocks)
+
+        def send(i, inner):
+            peer = block * sources + i
+
+            @pl.when(peer == me)
+            def _():
+                pltpu.make_async_copy(send_ref.at[me], x_all.at[me], recv_sems.at[me]).start()
+
+            @pl.when(peer != me)
+            def _():
+                remote(
+                    send_ref.at[peer], x_all.at[me], send_sems.at[peer], recv_sems.at[me], peer
+                ).start()
+
+            return inner
+
+        return lax.fori_loop(0, sources, send, carry)
+
+    lax.fori_loop(0, blocks, send_block, 0)
+
+    def work(j, wait_weights):
+        first_source = lax.rem(mine + j, blocks) * sources
+
+        def arrive(i, carry):
+            source = first_source + i
+            remote(
+                send_ref.at[source], x_all.at[source], send_sems.at[source], recv_sems.at[source],
+                source,
+            ).wait_recv()
+            return carry
+
+        lax.fori_loop(0, sources, arrive, 0)
+        x = x_all[pl.ds(first_source, sources)].reshape(rows, width)
+        halves = [ref[pl.ds(first_source, sources)] for ref in (ga_ref, gb_ref)]
+        g = jnp.concatenate(halves, axis=1).reshape(rows, width)
+
+        def first(f):
+            part = slice(f * sub, (f + 1) * sub)
+            if wait_weights:
+                for load in loads[f]:
+                    load.wait()
+            return nt(x, w_in[part]), nt(g, w_out[part])
+
+        def second(hidden, grad_activated):
+            activated, slope = gelu_parts(hidden)
+            return activated.astype(bf16), (grad_activated * slope).astype(bf16)
+
+        sums = None
+        ahead, behind = first(0), None
+        for f in range(count + 1):
+            now = ahead
+            if f + 1 < count:
+                ahead = first(f + 1)
+            if behind is not None:
+                part = slice((f - 1) * sub, f * sub)
+                terms = nn(behind[1], w_in[part]), nn(behind[0], w_out[part])
+                sums = terms if sums is None else (sums[0] + terms[0], sums[1] + terms[1])
+            if f < count:
+                behind = second(*now)
+        dims = (sources, capacity, width)
+        slots_all[pl.ds(first_source, sources)] = sums[0].astype(bf16).reshape(dims)
+        result_all[pl.ds(first_source, sources)] = sums[1].astype(bf16).reshape(dims)
+
+        def answer(i, carry):
+            peer = first_source + i
+
+            @pl.when(peer == me)
+            def _():
+                pltpu.make_async_copy(slots_all.at[me], back_ref.at[me], back_recv.at[me]).start()
+
+            @pl.when(peer != me)
+            def _():
+                remote(
+                    slots_all.at[peer], back_ref.at[me], back_sems.at[peer], back_recv.at[me], peer
+                ).start()
+
+            return carry
+
+        lax.fori_loop(0, sources, answer, 0)
+
+    work(0, True)
+
+    def later(j, carry):
+        work(j, False)
+        return carry
+
+    lax.fori_loop(1, blocks, later, 0)
+    keeps = [pltpu.make_async_copy(result_all, result_ref, keep_sems.at[0])]
+    for n, ref in enumerate((arrived_0, arrived_1, arrived_2, arrived_3)):
+        side, half = groups // 2, capacity // 2
+        part = x_all.at[pl.ds((n % 2) * side, side), pl.ds((n // 2) * half, half)]
+        keeps.append(pltpu.make_async_copy(part, ref, keep_sems.at[n + 1]))
+    for keep in keeps:
+        keep.start()
+
+    def close(peer, carry):
+        @pl.when(peer != me)
+        def _():
+            remote(
+                send_ref.at[peer], x_all.at[peer], send_sems.at[peer], recv_sems.at[peer], peer
+            ).wait_send()
+            remote(
+                slots_all.at[peer], back_ref.at[peer], back_sems.at[peer], back_recv.at[peer], peer
+            ).wait_send()
+
+        remote(
+            slots_all.at[peer], back_ref.at[peer], back_sems.at[peer], back_recv.at[peer], peer
+        ).wait_recv()
+        return carry
+
+    lax.fori_loop(0, groups, close, 0)
+    for keep in keeps:
+        keep.wait()
+
+
+def expert_main(send, ga, gb, w_in, w_out, rows=256, sub=512, after=()):
+    groups, capacity, width = send.shape
+    units = w_in.shape[0]
+    dma = pltpu.SemaphoreType.DMA
+    part = (groups // 2, capacity // 2, width)
+    return launch(
+        functools.partial(expert_kernel, rows=rows, sub=sub),
+        (send, ga, gb, w_in, w_out),
+        [ANY, whole(ga), whole(gb), ANY, ANY],
+        60,
+        after,
+        collective_id=1,
+        out_specs=[ANY] * 6,
+        out_shape=[shape(send.shape, bf16)] * 2 + [shape(part, bf16)] * 4,
+        scratch_shapes=[pltpu.VMEM((units, width), bf16)] * 2
+        + [pltpu.VMEM(send.shape, bf16)] * 3
+        + [dma((2, units // sub))]
+        + [dma((groups,))] * 4
+        + [dma((5,))],
+    )
+
+
+def expert_grad_kernel(x_ref, g_ref, in_ref, out_ref, *refs, sub, more):
+    gin_ref, gout_ref = refs[-2:]
+    copies = x_ref.shape[0]
+    order = [(r, p) for r in range(in_ref.shape[0] // sub) for p in range(copies)]
 
     def rows(r):
         return slice(r * sub, (r + 1) * sub)
 
     def first(r, p):
-        return nt(in_ref[rows(r)], x_refs[p][...]), nt(out_ref[rows(r)], g_refs[p][...])
+        return nt(in_ref[rows(r)], x_ref[p]), nt(out_ref[rows(r)], g_ref[p])
 
     def second(hidden, grad_activated):
         activated, slope = gelu_parts(hidden)
         return activated.astype(bf16), (grad_activated * slope).astype(bf16)
 
     def third(activated, grad_hidden, r, p):
-        grad_out = nn(activated, g_refs[p][...])
-        grad_in = nn(grad_hidden, x_refs[p][...])
-        if p:
-            grad_out += gout_ref[rows(r)]
-            grad_in += gin_ref[rows(r)]
+        grad_out = nn(activated, g_ref[p])
+        grad_in = nn(grad_hidden, x_ref[p])
+        if p or more:
+            before_in, before_out = (gin_ref, gout_ref) if p else refs[:2]
+            grad_in += before_in[rows(r)]
+            grad_out += before_out[rows(r)]
         gout_ref[rows(r)] = grad_out
         gin_ref[rows(r)] = grad_in
 
@@ -442,17 +674,29 @@
     third(*behind, *order[-1])
 
 
-def expert_grads(xs, gs, w_in, w_out, block=256, sub=256):
-    units, width = w_in.shape
+def expert_grads(x, g, side, w_in, w_out, before=(), block=256, sub=256, after=()):
+    copies, groups, half, width = g.shape
+    part_rows = groups * half // 2
+    x, g = (a.reshape(copies, -1, width) for a in (x, g))
+    units = w_in.shape[0]
     blocked = row_spec(block, width)
-    return pl.pallas_call(
-        functools.partial(expert_grad_kernel, count=len(xs), sub=sub),
+    return launch(
+        functools.partial(expert_grad_kernel, sub=sub, more=len(before) > 0),
+        (x, g, w_in, w_out, *before),
+        [
+            whole(x),
+            pl.BlockSpec((copies, part_rows, width), lambda i: (0, side, 0)),
+            blocked,
+            blocked,
+        ]
+        + [blocked] * len(before),
+        14,
+        after,
         grid=(units // block,),
-        in_specs=[whole(a) for a in (*xs, *gs)] + [blocked, blocked],
         out_specs=[blocked, blocked],
         out_shape=[shape((units, width), f32)] * 2,
-        compiler_params=params(),
-    )(*xs, *gs, w_in, w_out)
+        input_output_aliases={4: 0, 5: 1} if before else {},
+    )
 
 
 def back_kernel(
@@ -480,14 +724,14 @@
     gshift_ref[...] += jnp.sum(grad_sent, axis=0, keepdims=True)
 
 
-def middle_back(back, place, middle, cotangent, lengths, gain, w_output, block=256):
+def middle_back(back, place, middle, cotangent, lengths, gain, w_output, block=256, after=()):
     rows, width = middle.shape
     blocked = row_spec(block, width)
     vector = pl.BlockSpec((1, width), lambda i: (0, 0))
-    return pl.pallas_call(
+    return launch(
         back_kernel,
-        grid=(rows // block,),
-        in_specs=[
+        (back, place, middle, cotangent, lengths, gain, w_output,),
+        [
             whole(back),
             pl.BlockSpec((8, block), lambda i: (0, i)),
             blocked,
@@ -496,32 +740,67 @@
             whole(gain),
             whole(w_output),
         ],
+        12,
+        after,
+        grid=(rows // block,),
         out_specs=[blocked, blocked, blocked, vector, vector],
         out_shape=[shape((rows, width), f32)]
         + [shape((rows, width), bf16)] * 2
         + [shape((1, width), f32)] * 2,
-        compiler_params=params(),
-    )(back, place, middle, cotangent, lengths, gain, w_output)
-
-
-def weight_grad_kernel(a_ref, *refs, kind):
-    count = len(refs) // 2
+    )
+
+
+def weight_grad_kernel(a_ref, *refs):
     left = a_ref[...].T
-    for b_ref, o_ref in zip(refs[:count], refs[count:]):
-        o_ref[...] = nn(left, b_ref[...]).astype(kind)
-
-
-def weight_grads(a, bs, block=256, kind=bf16):
+    groups, _, _, share, width = refs[-1].shape
+    for n, b_ref in enumerate(refs[:-1]):
+        product = nn(left, b_ref[...]).reshape(groups, share, width)
+        refs[-1][:, 0, n] = product.astype(bf16)
+
+
+def weight_grads(a, bs, groups, copies, after=()):
     rows, width = a.shape
     out_width = bs[0].shape[1]
-    return pl.pallas_call(
-        functools.partial(weight_grad_kernel, kind=kind),
-        grid=(width // block,),
-        in_specs=[pl.BlockSpec((rows, block), lambda i: (0, i))] + [whole(b) for b in bs],
-        out_specs=[row_spec(block, out_width)] * len(bs),
-        out_shape=[shape((width, out_width), kind)] * len(bs),
-        compiler_params=params(),
-    )(a, *bs)
+    block = width // copies
+    dims = (groups, copies, len(bs), block // groups, out_width)
+    return launch(
+        weight_grad_kernel,
+        (a, *bs),
+        [pl.BlockSpec((rows, block), lambda i: (0, i))] + [whole(b) for b in bs],
+        4 * len(bs),
+        after,
+        grid=(copies,),
+        out_specs=pl.BlockSpec((groups, 1) + dims[2:], lambda i: (0, i, 0, 0, 0)),
+        out_shape=shape(dims, bf16),
+    )
+
+
+def near_add_kernel(*refs):
+    o_ref = refs[-1]
+    start = 0
+    for ref in refs[:-1]:
+        count = ref.shape[2]
+        o_ref[0, start : start + count] = jnp.sum(ref[:, 0].astype(f32), axis=0).astype(bf16)
+        start += count
+
+
+def near_add(parts, after=()):
+    copies = parts[0].shape[1]
+    dims = (sum(p.shape[2] for p in parts),) + parts[0].shape[3:]
+
+    def spec(p):
+        return pl.BlockSpec(p.shape[:1] + (1,) + p.shape[2:], lambda i: (0, i, 0, 0, 0))
+
+    return launch(
+        near_add_kernel,
+        tuple(parts),
+        [spec(p) for p in parts],
+        6,
+        after,
+        grid=(copies,),
+        out_specs=pl.BlockSpec((1,) + dims, lambda i: (i, 0, 0, 0)),
+        out_shape=shape((copies,) + dims, bf16),
+    )
 
 
 def input_back_kernel(
@@ -543,18 +822,20 @@
     gshift_ref[...] += jnp.sum(grad_normed, axis=0, keepdims=True)
 
 
-def input_back(gq, gk, gv, wq, wk, wv, x, grad_middle, gain, block=256):
+def input_back(gq, gk, gv, wq, wk, wv, x, grad_middle, gain, block=256, after=()):
     rows, width = x.shape
     blocked = row_spec(block, width)
     vector = pl.BlockSpec((1, width), lambda i: (0, 0))
-    return pl.pallas_call(
+    return launch(
         input_back_kernel,
+        (gq, gk, gv, wq, wk, wv, x, grad_middle, gain,),
+        [blocked] * 3 + [whole(w) for w in (wq, wk, wv)] + [blocked, blocked, whole(gain)],
+        14,
+        after,
         grid=(rows // block,),
-        in_specs=[blocked] * 3 + [whole(w) for w in (wq, wk, wv)] + [blocked, blocked, whole(gain)],
         out_specs=[blocked, vector, vector],
         out_shape=[shape((rows, width), f32)] + [shape((1, width), f32)] * 2,
-        compiler_params=params(),
-    )(gq, gk, gv, wq, wk, wv, x, grad_middle, gain)
+    )
 
 
 def output_kernel(back_ref, place_ref, mid_ref, o_ref):
@@ -562,20 +843,22 @@
     o_ref[...] = (mid_ref[...] + combined).astype(bf16)
 
 
-def combine(back, place, middle, block=256):
+def combine(back, place, middle, block=256, after=()):
     rows, width = middle.shape
-    return pl.pallas_call(
+    return launch(
         output_kernel,
-        grid=(rows // block,),
-        in_specs=[
+        (back, place, middle,),
+        [
             whole(back),
             pl.BlockSpec((8, block), lambda i: (0, i)),
             row_spec(block, width),
         ],
+        7,
+        after,
+        grid=(rows // block,),
         out_specs=row_spec(block, width),
         out_shape=shape((rows, width), bf16),
-        compiler_params=params(),
-    )(back, place, middle)
+    )
 
 
 def body(
@@ -611,70 +894,65 @@
     table = jnp.pad(hash_table, (0, table_rows * 128 - hash_table.shape[0]))
     table = table.reshape(table_rows, 128)
 
-    def exchange(array):
-        return lax.all_to_all(
-            array.reshape(groups, capacity, width), "exp", split_axis=0, concat_axis=0, tiled=True
-        ).reshape(slot_total, width)
-
-    def spread(array):
-        up, down = [array], [array]
-        for _ in range(copies - 1):
-            up.append(lax.ppermute(up[-1], "rep", [(i, i + 1) for i in range(copies - 1)]))
-            down.append(lax.ppermute(down[-1], "rep", [(i + 1, i) for i in range(copies - 1)]))
-        return [
-            jnp.where(place_z >= step, up[step], down[copies - step]) for step in range(1, copies)
-        ]
-
-    place, grad_send = route(
-        lengths, token_ids.reshape(1, rows), table, cot, groups, capacity
-    )
-    grad_arrived = exchange(grad_send)
-    normed, q, k, v = project(x, gain_one, shift_one, w_query, w_key, w_value)
-    mixed, logs = attend(lengths, q, k, v)
-    middle, send_rows = middle_and_send(x, mixed, w_output, gain_two, shift_two, place, slot_total)
-    arrived = exchange(send_rows)
-    grad_slots, activated = expert_main(arrived, grad_arrived, expert_in[0], expert_out[0])
-    grad_back = exchange(grad_slots)
-    returned = exchange(expert_result(activated, expert_out[0]))
+    def gather(array):
+        return lax.all_gather(array, "rep", axis=0, tiled=False)
+
+    def near(parts):
+        return lax.all_to_all(parts, "exp", split_axis=0, concat_axis=0, tiled=True)
+
+    def far_sum(parts):
+        far = lax.all_to_all(parts, "rep", split_axis=0, concat_axis=0, tiled=True)
+        return jnp.sum(far.astype(f32), axis=0)
+
+    place, send_a, send_b = route(lengths, token_ids.reshape(1, rows), table, cot, groups, capacity)
+    normed, q, k, v, cot_a = project(x, gain_one, shift_one, w_query, w_key, w_value, send_a)
+    cots_a = gather(cot_a)
+    mixed, logs, cot_b = attend(lengths, q, k, v, send_b)
+    cots_b = gather(cot_b)
+    middle, send_rows = middle_and_send(
+        x, mixed, w_output, gain_two, shift_two, place, slot_total, after=(cot_b,)
+    )
+    grad_back, result, *arrived = expert_main(
+        send_rows.reshape(groups, capacity, width), cot_a, cot_b, expert_in[0], expert_out[0]
+    )
+    sent = [gather(a) for a in arrived]
     grad_middle, branch, grad_mixed, grad_second_gain, grad_second_shift = middle_back(
-        grad_back, place, middle, cot, lengths, gain_two, w_output
-    )
-    (grad_w_output,) = weight_grads(mixed, [branch])
-    gq, gk, gv = attend_back(lengths, q, k, v, mixed, grad_mixed, logs)
-    grad_qkv = weight_grads(normed, [gq, gk, gv])
+        grad_back.reshape(slot_total, width), place, middle, cot, lengths, gain_two, w_output
+    )
+    parts_output = weight_grads(mixed, [branch], groups, copies, after=(cots_a,))
+    gq, gk, gv, returned = attend_back(
+        lengths, q, k, v, mixed, grad_mixed, logs, result, after=(parts_output,)
+    )
+    near_output = near(parts_output)
     grad_inputs, grad_first_gain, grad_first_shift = input_back(
         gq, gk, gv, w_query, w_key, w_value, x, grad_middle, gain_one
     )
-    outputs = combine(returned, place, middle)
+    parts_qkv = weight_grads(normed, [gq, gk, gv], groups, copies, after=(grad_first_gain,))
+    near_qkv = near(parts_qkv)
+    outputs = combine(
+        returned.reshape(slot_total, width), place, middle, after=(parts_qkv, cots_b)
+    )
+    devices = groups * copies
+    vectors = jnp.concatenate(
+        [grad_first_gain, grad_first_shift, grad_second_gain, grad_second_shift], axis=0
+    )
+    vectors = vectors.reshape(4, devices, width // devices).transpose(1, 0, 2)
+    vectors = lax.all_to_all(vectors, ("rep", "exp"), split_axis=0, concat_axis=0, tiled=True)
+    vectors = jnp.sum(vectors, axis=0)
 
     share = expert_in.shape[1] // copies
     shares = [
         lax.dynamic_slice_in_dim(w[0], place_z * share, share, axis=0)
         for w in (expert_in, expert_out)
     ]
-    grad_expert_in, grad_expert_out = expert_grads(
-        [arrived, *spread(arrived)], [grad_arrived, *spread(grad_arrived)], *shares
-    )
-
-    def scatter(arrays):
-        devices = groups * copies
-        parts = [a.reshape(copies, groups, width // devices, width) for a in arrays]
-        joined = jnp.concatenate(parts, axis=2)
-        joined = lax.psum_scatter(
-            joined.transpose(1, 0, 2, 3), "exp", scatter_dimension=0, tiled=True
-        )
-        joined = lax.psum_scatter(joined[0], "rep", scatter_dimension=0, tiled=True)[0]
-        return [part.astype(f32) for part in jnp.split(joined, len(arrays), axis=0)]
-
-    (dense_output,) = scatter([grad_w_output])
-    dense_query, dense_key, dense_value = scatter(grad_qkv)
-    vectors = jnp.concatenate(
-        [grad_first_gain, grad_first_shift, grad_second_gain, grad_second_shift], axis=0
-    )
-    vectors = lax.psum(vectors, ("rep", "exp"))
-    part = width // (groups * copies)
-    mine = (place_z * groups + lax.axis_index("exp")) * part
-    vectors = lax.dynamic_slice_in_dim(vectors, mine, part, axis=1)
+    sums = expert_grads(sent[0], cots_a, 0, *shares, after=(outputs,))
+    sums = expert_grads(sent[1], cots_a, 1, *shares, before=sums)
+    near_all = near_add([near_output, near_qkv], after=(sums[0],))
+    dense = far_sum(near_all)
+    sums = expert_grads(sent[2], cots_b, 0, *shares, before=sums, after=(near_all, vectors))
+    sums = expert_grads(sent[3], cots_b, 1, *shares, before=sums, after=(dense,))
+    grad_expert_in, grad_expert_out = sums
+    dense_output, dense_query, dense_key, dense_value = dense
     return (
         outputs.reshape(seq_count, seq_len, width),
         grad_inputs.reshape(seq_count, seq_len, width),

time: 722 us -> 424 us (0.59)
  blocking collectives: 170 us -> 11.3 us
  waiting for transfers between devices: 224 us -> 95.7 us
  Pallas kernels: 220 us -> 269 us
  starting transfers between devices: 40.5 us -> 12.6 us
  other arithmetic: 29 us -> 1.64 us
    ppermute x12 -> x0, waiting for transfers between devices: 210 us -> none  [the longest x6 141 us: spread(): lax.ppermute(down[-1], 'rep', [(i + 1, i) for i in range(copies - 1)])]
    all_to_all x3 -> x1, blocking collectives: 92.9 us -> 11.3 us  [body(): lax.all_to_all(vectors, ('rep', 'exp'), split_axis=0, concat_axis=0, tile...]
    psum x1 -> x0, blocking collectives: 77.4 us -> none  [body(): vectors = lax.psum(vectors, ('rep', 'exp'))]
    all_gather x0 -> x6, waiting for transfers between devices: none -> 68.9 us  [gather(): return lax.all_gather(array, 'rep', axis=0, tiled=False)]
    pallas_call x13 -> x16, Pallas kernels: 220 us -> 269 us  [launch(): pl.pallas_call(run, in_specs=list(in_specs) + [pl.BlockSpec(memory_space=...]
    ppermute x12 -> x0, starting transfers between devices: 36.5 us -> none  [the longest x6 28.5 us: spread(): lax.ppermute(up[-1], 'rep', [(i, i + 1) for i in range(copies - 1)])]
    all_to_all x1 -> x3, waiting for transfers between devices: 0.01 us -> 25.2 us  [the longest x2 24.4 us: near(): return lax.all_to_all(parts, 'exp', split_axis=0, concat_axis=0, tiled=True)]
    select_n x6 -> x0, other arithmetic: 19.1 us -> none  [spread(): jnp.where(place_z >= step, up[step], down[copies - step])]
  transfers between devices with their start and end apart: 17 -> 9, of which waited for: 7 -> 6; matrix products, arithmetic and copies ran while one was open for 5% -> 2% of each run, Pallas kernels for 17% -> 55%
where the time goes in v2:
time: 424 us; the launch traced here: 416 us
  Pallas kernels  269 us (63%)
  waiting for transfers between devices  95.7 us (23%)
  between operations  15.4 us (4%)
  starting transfers between devices  12.6 us (3%)
  blocking collectives  11.3 us (3%)
  local copies, waits for them, and re-layouts  9.58 us (2%)
    pallas_call x16, Pallas kernels, launch(): pl.pallas_call(run, in_specs=list(in_specs) + [pl.BlockSpec(memory_space=...  269 us
    all_gather x6, waiting for transfers between devices, gather(): return lax.all_gather(array, 'rep', axis=0, tiled=False)  68.9 us
    all_to_all x2, waiting for transfers between devices, near(): return lax.all_to_all(parts, 'exp', split_axis=0, concat_axis=0, tiled=True)  24.4 us
    all_to_all x1, blocking collectives, body(): lax.all_to_all(vectors, ('rep', 'exp'), split_axis=0, concat_axis=0, tile...  11.3 us
    all_to_all x2, starting transfers between devices, near(): return lax.all_to_all(parts, 'exp', split_axis=0, concat_axis=0, tiled=True)  8.59 us
  transfers between devices with their start and end apart: 9, of which 6 were waited for; matrix products, arithmetic and copies ran while one was open for 2% of the time, Pallas kernels for 55%

profile of v2, /device:TPU:0, one launch (start us, length us, event | category | flops | bytes accessed | tf_op | source)
XLA Modules:
  0.0 415.7 jit_solution(16773844086485403589)
XLA Ops:
  7.9 1.4 pad_bitcast_fusion.refs_2_
  9.2 5.7 %shard_map.238 = (f32[8,1024]{1,0:T(8,128)}, bf16[8,64,1024]{2,1,0:T(8,128)(2,1)}, bf16[8,64,1024]{2,1,0:T(8,128)(2,1)}) custom-call(s32[1]{0:T(128)S(6)} %copy.42.refs_0_.refs_4_, s32[1,1024]{1,0:T(1,128)} %refs_1_.1, s32[64,128]{1,0:T(8,128)} %pad_bitcast_fusion.refs_2_, bf16[1024,1024]{1,0:T(8,128)(2,1)} %bitcast.57), custom_call_target="tpu_custom_call" | custom-call | flops 11000000512 | bytes 35000000 | tf_op jit(solution)/shard_map/pallas_call | solution.py:36
  14.9 20.5 %shard_map.239 = (bf16[1024,1024]{1,0:T(8,128)(2,1)}, bf16[1024,1024]{1,0:T(8,128)(2,1)}, bf16[1024,1024]{1,0:T(8,128)(2,1)}, bf16[1024,1024]{1,0:T(8,128)(2,1)}, bf16[8,64,1024]{2,1,0:T(8,128)(2,1)}) custom-call(bf16[1024,1024]{1,0:T(8,128)(2,1)} %bitcast.59, f32[1,1024]{1,0:T(1,128)} %bitcast.70, f32[1,1024]{1,0:T(1,128)} %bitcast.66, ...), custom_call_target="tpu_custom_call" | custom-call | flops 17600000000 | bytes 56000000 | tf_op jit(solution)/shard_map/pallas_call | solution.py:36
  35.5 20.6 %shard_map.240 = (bf16[1024,1024]{1,0:T(8,128)(2,1)}, f32[8,2,1024]{2,1,0:T(2,128)}, bf16[8,64,1024]{2,1,0:T(8,128)(2,1)}) custom-call(s32[1]{0:T(128)S(6)} %copy.42.refs_0_.refs_4_, bf16[1024,1024]{1,0:T(8,128)(2,1)} %get-tuple-element.52.refs_1_, bf16[1024,1024]{1,0:T(8,128)(2,1)} %get-tuple-element.53.refs_2_, ...), custom_call_target="tpu_custom_call" | custom-call | flops 26400000000 | bytes 84000000 | tf_op jit(solution)/shard_map/pallas_call | solution.py:36
  56.2 10.7 %shard_map.241 = (f32[1024,1024]{1,0:T(8,128)}, bf16[1024,1024]{1,0:T(8,128)(2,1)}) custom-call(bf16[1024,1024]{1,0:T(8,128)(2,1)} %bitcast.60, bf16[1024,1024]{1,0:T(8,128)(2,1)} %get-tuple-element.56.refs_1_.refs_0_.refs_4_, bf16[1024,1024]{1,0:T(8,128)(2,1)} %refs_6_.1, f32[1,1024]{1,0:T(1,128)} %bitcast.68, f32[1,1024]{1,0:T(1,128)} %bitcast.67, ...), custom_call_target="tpu_custom_call" | custom-call | flops 11000000512 | bytes 35000000 | tf_op jit(solution)/shard_map/pallas_call | solution.py:36
  67.0 60.6 %shard_map.242 = (bf16[8,128,1024]{2,1,0:T(8,128)(2,1)}, bf16[8,128,1024]{2,1,0:T(8,128)(2,1)}, bf16[4,64,1024]{2,1,0:T(8,128)(2,1)}, bf16[4,64,1024]{2,1,0:T(8,...) custom-call(bf16[8,128,1024]{2,1,0:T(8,128)(2,1)} %bitcast.78, ...), custom_call_target="tpu_custom_call" | custom-call | flops 65999998976 | bytes 210000000 | tf_op jit(solution)/shard_map/pallas_call | solution.py:36
  128.2 12.8 %shard_map.243 = (f32[1024,1024]{1,0:T(8,128)}, bf16[1024,1024]{1,0:T(8,128)(2,1)}, bf16[1024,1024]{1,0:T(8,128)(2,1)}, f32[1,1024]{1,0:T(1,128)}, f32[1,1024]{1,0:T(1,128)}) custom-call(bf16[1024,1024]{1,0:T(8,128)(2,1)} %bitcast.77, f32[8,1024]{1,0:T(8,128)} %get-tuple-element.57.refs_5_.refs_1_, f32[1024,1024]{1,0:T(8,128)} %get-tuple-element.62.refs_2_, ...), custom_call_target="tpu_custom_call" | custom-call | flops 13200000000 | bytes 42000000 | tf_op jit(solution)/shard_map/pallas_call | solution.py:36
  141.0 6.1 %shard_map.244.refs_8_ = bf16[8,4,1,32,1024]{4,3,2,1,0:T(8,128)(2,1)} custom-call(bf16[1024,1024]{1,0:T(8,128)(2,1)} %get-tuple-element.56.refs_1_.refs_0_.refs_4_, bf16[1024,1024]{1,0:T(8,128)(2,1)} %get-tuple-element.66.refs_1_, bf16[4,8,64,1024]{3,2,1,0:T(8,128)(2,1)} %bitcast.54), custom_call_target="tpu_custom_call" | custom-call | flops 4400000000 | bytes 14000000 | tf_op jit(solution)/shard_map/pallas_call | solution.py:36
  147.1 35.5 %shard_map.245 = (bf16[1024,1024]{1,0:T(8,128)(2,1)}, bf16[1024,1024]{1,0:T(8,128)(2,1)}, bf16[1024,1024]{1,0:T(8,128)(2,1)}, bf16[8,128,1024]{2,1,0:T(8,128)(2,1)}) custom-call(s32[1]{0:T(128)S(6)} %copy.42.refs_0_.refs_4_, bf16[1024,1024]{1,0:T(8,128)(2,1)} %get-tuple-element.52.refs_1_, bf16[1024,1024]{1,0:T(8,128)(2,1)} %get-tuple-element.53.refs_2_, ...), custom_call_target="tpu_custom_call" | custom-call | flops 34100000768 | bytes 108500000 | tf_op jit(solution)/shard_map/pallas_call | solution.py:36
  182.6 14.5 %shard_map.246 = (f32[1024,1024]{1,0:T(8,128)}, f32[1,1024]{1,0:T(1,128)}, f32[1,1024]{1,0:T(1,128)}) custom-call(bf16[1024,1024]{1,0:T(8,128)(2,1)} %get-tuple-element.69.refs_0_.refs_1_, bf16[1024,1024]{1,0:T(8,128)(2,1)} %get-tuple-element.70.refs_1_.refs_2_, bf16[1024,1024]{1,0:T(8,128)(2,1)} %get-tuple-element.71.refs_2_.refs_3_, ...), custom_call_target="tpu_custom_call" | custom-call | flops 15399999488 | bytes 49000000 | tf_op jit(solution)/shard_map/pallas_call | solution.py:36
  197.1 0.7 pad_maximum_fusion
  198.1 11.3 %all_to_all.20 = f32[32,1,128]{2,1,0:T(1,128)S(1)} all-to-all(f32[32,1,128]{2,1,0:T(1,128)S(1)} %reshape.116), channel_id=1, replica_groups=mesh['rep'=4,'exp'=8] {'rep','exp'}, dimensions={0} | all-to-all | bytes 32768 | tf_op jit(solution)/shard_map/all_to_all | solution.py:940
  209.4 3.9 all-to-all-start.1
  213.8 11.7 %shard_map.247.refs_3_ = bf16[8,4,3,32,1024]{4,3,2,1,0:T(8,128)(2,1)} custom-call(bf16[1024,1024]{1,0:T(8,128)(2,1)} %get-tuple-element.68.refs_0_, bf16[1024,1024]{1,0:T(8,128)(2,1)} %get-tuple-element.69.refs_0_.refs_1_, bf16[1024,1024]{1,0:T(8,128)(2,1)} %get-tuple-element.70.refs_1_.refs_2_, bf16[1024,1024]{1,0:T(8,128)(2,1)} %get-tuple-element.71.refs_2_.refs_3_, ...), custom_call_target="tpu_custom_call" | custom-call | flops 13200000000 | bytes 42000000 | tf_op jit(solution)/shard_map/pallas_call | solution.py:36
  225.5 14.3 %all-to-all-done.1.refs_0_ = bf16[8,4,1,32,1024]{4,3,2,1,0:T(8,128)(2,1)S(1)} async-done(((bf16[8,4,1,32,1024]{4,3,2,1,0:T(8,128)(2,1)}), bf16[8,4,1,32,1024]{4,3,2,1,0:T(8,128)(2,1)S(1)}, u32[]{:S(2)}, u32[]{:S(2)}) %all-to-all-start.1) | async-done | bytes 2097184 | tf_op jit(solution)/shard_map/all_to_all | solution.py:901
  239.8 1.3 copy-done.1
  241.2 4.7 %all-to-all-start.2 = ((bf16[8,4,3,32,1024]{4,3,2,1,0:T(8,128)(2,1)}), bf16[8,4,3,32,1024]{4,3,2,1,0:T(8,128)(2,1)}, u32[]{:S(2)}, u32[]{:S(2)}) async-start(bf16[8,4,3,32,1024]{4,3,2,1,0:T(8,128)(2,1)} %shard_map.247.refs_3_), calls=%async_computation.2 | async-start | bytes 12582912 | tf_op jit(solution)/shard_map/all_to_all | solution.py:901
  246.5 4.6 %dynamic-slice_bitcast_fusion = (bf16[1024,1024]{1,0:T(8,128)(2,1)}, bf16[1024,1024]{1,0:T(8,128)(2,1)}) fusion(bf16[1,4096,1024]{2,1,0:T(8,128)(2,1)} %param.29, s32[]{:T(128)S(6)} %select_n.4, bf16[1,4096,1024]{2,1,0:T(8,128)(2,1)} %param.28), kind=kLoop, calls=%fused_computation.1 | loop fusion | bytes 8388612 | tf_op jit(solution)/shard_map/dynamic_slice | solution.py:945
  251.1 7.2 %shard_map.248.refs_4_ = bf16[1024,1024]{1,0:T(8,128)(2,1)} custom-call(bf16[1024,1024]{1,0:T(8,128)(2,1)} %bitcast.76, f32[8,1024]{1,0:T(8,128)} %get-tuple-element.57.refs_5_.refs_1_, f32[1024,1024]{1,0:T(8,128)} %get-tuple-element.62.refs_2_, bf16[8,4,3,32,1024]{4,3,2,1,0:T(8,128)(2,1)} %shard_map.247.refs_3_, bf16[4,8,64,1024]{3,2,1,0:T(8,128)(2,1)} %bitcast.51), custom_call_target="tpu_custom_call" | custom-call | flops 7699999744 | bytes 24500000 | tf_op jit(solution)/shard_map/pallas_call | solution.py:36
  258.3 14.0 %shard_map.249 = (f32[1024,1024]{1,0:T(8,128)}, f32[1024,1024]{1,0:T(8,128)}) custom-call(bf16[4,256,1024]{2,1,0:T(8,128)(2,1)} %bitcast.62, bf16[4,512,1024]{2,1,0:T(8,128)(2,1)} %bitcast.55, bf16[1024,1024]{1,0:T(8,128)(2,1)} %get-tuple-element.99.refs_2_, bf16[1024,1024]{1,0:T(8,128)(2,1)} %get-tuple-element.98.refs_3_, bf16[1024,1024]{1,0:T(8,128)(2,1)} %shard_map.248.refs_4_), custom_call_target="tpu_custom_call" | custom-call | flops 15399999488 | bytes 49000000 | tf_op jit(solution)/shard_map/pallas_call | solution.py:36
  272.4 19.0 %all-gather.17.cloned.1.call-done = bf16[16,64,1024]{2,1,0:T(8,128)(2,1)} async-done(((bf16[4,64,1024]{2,1,0:T(8,128)(2,1)}), bf16[16,64,1024]{2,1,0:T(8,128)(2,1)}) %all-gather.17.cloned.1.call-update) | async-done | bytes 2097168 | tf_op jit(solution)/shard_map/all_gather | solution.py:898
  291.3 14.7 %shard_map.250 = (f32[1024,1024]{1,0:T(8,128)}, f32[1024,1024]{1,0:T(8,128)}) custom-call(bf16[4,256,1024]{2,1,0:T(8,128)(2,1)} %bitcast.63, bf16[4,512,1024]{2,1,0:T(8,128)(2,1)} %bitcast.56, bf16[1024,1024]{1,0:T(8,128)(2,1)} %get-tuple-element.99.refs_2_, ...), custom_call_target="tpu_custom_call", output_to_operand_aliasing={{0}: (4, {}), {1}: (5, {})} | custom-call | flops 15399999488 | bytes 49000000 | tf_op jit(solution)/shard_map/pallas_call | solution.py:36
  306.6 0.7 reduce
  307.4 10.1 %all-to-all-done.2.refs_1_ = bf16[8,4,3,32,1024]{4,3,2,1,0:T(8,128)(2,1)} async-done(((bf16[8,4,3,32,1024]{4,3,2,1,0:T(8,128)(2,1)}), bf16[8,4,3,32,1024]{4,3,2,1,0:T(8,128)(2,1)}, u32[]{:S(2)}, u32[]{:S(2)}) %all-to-all-start.2) | async-done | bytes 6291488 | tf_op jit(solution)/shard_map/all_to_all | solution.py:901
  317.5 5.3 %shard_map.251.refs_6_ = bf16[4,4,32,1024]{3,2,1,0:T(8,128)(2,1)} custom-call(bf16[8,4,1,32,1024]{4,3,2,1,0:T(8,128)(2,1)} %copy-done.1, bf16[8,4,3,32,1024]{4,3,2,1,0:T(8,128)(2,1)} %all-to-all-done.2.refs_1_, f32[1024,1024]{1,0:T(8,128)} %get-tuple-element.82.refs_2_.refs_4_), custom_call_target="tpu_custom_call" | custom-call | flops 6600000000 | bytes 21000000 | tf_op jit(solution)/shard_map/pallas_call | solution.py:36
  322.8 3.8 all-to-all-start.3
  327.2 20.7 %all-gather.23.cloned.1.call-done = bf16[16,64,1024]{2,1,0:T(8,128)(2,1)} async-done(((bf16[4,64,1024]{2,1,0:T(8,128)(2,1)}), bf16[16,64,1024]{2,1,0:T(8,128)(2,1)}) %all-gather.23.cloned.1.call-update) | async-done | bytes 2097168 | tf_op jit(solution)/shard_map/all_gather | solution.py:898
  347.9 14.7 %shard_map.252 = (f32[1024,1024]{1,0:T(8,128)}, f32[1024,1024]{1,0:T(8,128)}) custom-call(bf16[4,256,1024]{2,1,0:T(8,128)(2,1)} %bitcast.64, bf16[4,512,1024]{2,1,0:T(8,128)(2,1)} %bitcast.52, bf16[1024,1024]{1,0:T(8,128)(2,1)} %get-tuple-element.99.refs_2_, ...), custom_call_target="tpu_custom_call", output_to_operand_aliasing={{0}: (4, {}), {1}: (5, {})} | custom-call | flops 15399999488 | bytes 49000000 | tf_op jit(solution)/shard_map/pallas_call | solution.py:36
  362.6 0.8 all-to-all-done.3
  363.6 0.8 slice_bitcast_fusion
  364.4 29.2 %all-gather.21.cloned.1.call-done = bf16[16,64,1024]{2,1,0:T(8,128)(2,1)} async-done(((bf16[4,64,1024]{2,1,0:T(8,128)(2,1)}), bf16[16,64,1024]{2,1,0:T(8,128)(2,1)}) %all-gather.21.cloned.1.call-update) | async-done | bytes 2097168 | tf_op jit(solution)/shard_map/all_gather | solution.py:898
  393.7 14.7 %shard_map.253 = (f32[1024,1024]{1,0:T(8,128)}, f32[1024,1024]{1,0:T(8,128)}) custom-call(bf16[4,256,1024]{2,1,0:T(8,128)(2,1)} %bitcast.65, bf16[4,512,1024]{2,1,0:T(8,128)(2,1)} %bitcast.53, bf16[1024,1024]{1,0:T(8,128)(2,1)} %get-tuple-element.99.refs_2_, ...), custom_call_target="tpu_custom_call", output_to_operand_aliasing={{0}: (4, {}), {1}: (5, {})} | custom-call | flops 15399999488 | bytes 49000000 | tf_op jit(solution)/shard_map/pallas_call | solution.py:36
  (32 shorter events, 3.5 us)
Async XLA Ops:
  7.2 133.8 %all-gather.13.cloned.1.call-start = ((), (), s32[]{:S(2)}) async-start(), calls=%async_computation.4 | async-start | bytes 5242880 | tf_op jit(solution)/shard_map/all_gather | solution.py:898
  35.5 215.6 %all-gather.15.cloned.1.call-start = ((), (), s32[]{:S(2)}) async-start(), calls=%async_computation.5 | async-start | bytes 5242880 | tf_op jit(solution)/shard_map/all_gather | solution.py:898
  56.2 202.2 %all-gather.19.cloned.1.call-start = ((), (), s32[]{:S(2)}) async-start(), calls=%async_computation.7 | async-start | bytes 2621440 | tf_op jit(solution)/shard_map/all_gather | solution.py:898
  127.6 163.7 %all-gather.17.cloned.1.call-start = ((), (), s32[]{:S(2)}) async-start(), calls=%async_computation.6 | async-start | bytes 2621440 | tf_op jit(solution)/shard_map/all_gather | solution.py:898
  182.6 14.5 %copy-start.3 = (f32[1,1024]{1,0:T(1,128)S(1)}, f32[1,1024]{1,0:T(1,128)}, u32[]{:S(2)}) copy-start(f32[1,1024]{1,0:T(1,128)} %get-tuple-element.76) | copy-start | bytes 12292
  182.6 14.5 %copy-start.4 = (f32[1,1024]{1,0:T(1,128)S(1)}, f32[1,1024]{1,0:T(1,128)}, u32[]{:S(2)}) copy-start(f32[1,1024]{1,0:T(1,128)} %get-tuple-element.77) | copy-start | bytes 12292
  209.4 30.4 %all-to-all-start.1 = ((bf16[8,4,1,32,1024]{4,3,2,1,0:T(8,128)(2,1)}), bf16[8,4,1,32,1024]{4,3,2,1,0:T(8,128)(2,1)S(1)}, u32[]{:S(2)}, u32[]{:S(2)}) async-start(bf16[8,4,1,32,1024]{4,3,2,1,0:T(8,128)(2,1)} %shard_map.244.refs_8_), calls=%async_computation.1 | async-start | bytes 4194304 | tf_op jit(solution)/shard_map/all_to_all | solution.py:901
  213.2 134.6 %all-gather.23.cloned.1.call-start = ((), (), s32[]{:S(2)}) async-start(), calls=%async_computation.9 | async-start | bytes 2621440 | tf_op jit(solution)/shard_map/all_gather | solution.py:898
  239.8 1.3 copy-start.1
  241.2 76.3 %all-to-all-start.2 = ((bf16[8,4,3,32,1024]{4,3,2,1,0:T(8,128)(2,1)}), bf16[8,4,3,32,1024]{4,3,2,1,0:T(8,128)(2,1)}, u32[]{:S(2)}, u32[]{:S(2)}) async-start(bf16[8,4,3,32,1024]{4,3,2,1,0:T(8,128)(2,1)} %shard_map.247.refs_3_), calls=%async_computation.2 | async-start | bytes 12582912 | tf_op jit(solution)/shard_map/all_to_all | solution.py:901
  245.9 147.8 %all-gather.21.cloned.1.call-start = ((), (), s32[]{:S(2)}) async-start(), calls=%async_computation.8 | async-start | bytes 2621440 | tf_op jit(solution)/shard_map/all_gather | solution.py:898
  307.4 19.3 %copy-start.2 = (f32[4,32]{1,0:T(4,128)}, f32[4,32]{1,0:T(4,128)S(1)}, u32[]{:S(2)}) copy-start(f32[4,32]{1,0:T(4,128)S(1)} %reduce_sum.18.refs_7_) | copy-start | bytes 1540
  322.8 40.6 %all-to-all-start.3 = ((bf16[4,4,32,1024]{3,2,1,0:T(8,128)(2,1)}), bf16[4,4,32,1024]{3,2,1,0:T(8,128)(2,1)S(1)}, u32[]{:S(2)}, u32[]{:S(2)}) async-start(bf16[4,4,32,1024]{3,2,1,0:T(8,128)(2,1)} %shard_map.251.refs_6_), calls=%async_computation.3 | async-start | bytes 2097152 | tf_op jit(solution)/shard_map/all_to_all | solution.py:904
  363.6 30.1 %copy-start = (f32[4,32,1024]{2,1,0:T(8,128)}, f32[4,32,1024]{2,1,0:T(8,128)S(1)}, u32[]{:S(2)}) copy-start(f32[4,32,1024]{2,1,0:T(8,128)S(1)} %convert_reduce_fusion.refs_6_) | copy-start | bytes 1572868
Sparse Core Ops, SparseCore 0:
  35.6 82.4 all-gather.12
  119.6 79.2 all-gather.14
  200.5 44.4 all-gather.18
  246.5 44.8 all-gather.16
  292.7 55.0 all-gather.22
  349.3 44.3 all-gather.20
